TPU v7x, 512 devices: a whole 4x8x8 slice. The times are simulated.
512 devices in a mesh: dp: 64 (over y_hi, x, z), tensor: 8 (over y_lo, core).
Axes of the slice: x: 4, y: 8 (y_hi: 2, y_lo: 4; y = y_hi * 4 + y_lo), z: 8, core: 2. Of those that a mesh axis runs over, the one named last changes fastest.
Arguments:
- tokens: bfloat16 [49152, 4096], P(('dp', 'tensor')), may hold values from -6 to 6
- up_cotangent: bfloat16 [49152, 14336], P('dp', 'tensor'), may hold values from -6 to 6
- basis: bfloat16 [4096, 512], P('dp'), may hold values from -0.09375 to 0.09375
- first_moment: float32 [512, 14336], P('dp', 'tensor'), may hold values from -0.001953125 to 0.001953125
- second_moment: float32 [512, 14336], P('dp', 'tensor'), may hold values from 4.0871757e-11 to 4.0871756e-10
Outputs:
- update: float32 [4096, 14336], P('dp', 'tensor')
All inputs are finite; a program needn't handle non-finite values.
Results may differ from a plain program's by a relative error of at most 0.0032.
Values may be sent and summed in bfloat16 or wider, within the bound.
A program may use at most 64 MiB of HBM per device.

v0:
```python
import jax
import jax.numpy as jnp
from jax import lax
from jax.sharding import PartitionSpec as P


def local(tokens, up_cotangent, basis, first_moment, second_moment):
    share = first_moment.shape[0]
    columns = tokens
    projected = jnp.dot(
        columns, lax.all_gather(basis, "dp", axis=0, tiled=True), preferred_element_type=jnp.float32
    ).astype(jnp.bfloat16)
    replica = lax.all_gather(projected, "tensor", axis=0, tiled=True)
    count = float(replica.shape[0] * lax.axis_size("dp"))
    product = lax.dot_general(
        replica, up_cotangent, (((0,), (0,)), ((), ())), preferred_element_type=jnp.float32
    )
    summed = lax.psum(product / count, "dp")
    squares = lax.psum(jnp.sum(summed * summed), "tensor")
    grad = lax.dynamic_slice_in_dim(summed, lax.axis_index("dp") * share, share, 0)
    norm = jnp.sqrt(squares)
    clipped = grad * jnp.minimum(1.0, 1.0 / norm)
    new_first = 0.9 * first_moment + 0.1 * clipped
    new_second = 0.999 * second_moment + 0.001 * clipped * clipped
    first_fix = 1.0 - 0.9**20
    second_fix = 1.0 - 0.999**20
    direction = (new_first / first_fix / (jnp.sqrt(new_second / second_fix) + 1e-08)).astype(
        jnp.bfloat16
    )
    columns = basis
    return jnp.dot(
        columns,
        lax.all_gather(direction, "dp", axis=0, tiled=True),
        preferred_element_type=jnp.float32,
    )


def solution(mesh):
    in_specs = (
        P(("dp", "tensor"), None),
        P("dp", "tensor"),
        P("dp", None),
        P("dp", "tensor"),
        P("dp", "tensor"),
    )
    out_specs = P("dp", "tensor")
    return jax.shard_map(local, mesh=mesh, in_specs=in_specs, out_specs=out_specs, check_vma=False)
```

profile of v0, /device:TPU:8, one launch (start us, length us, event | category | flops | bytes accessed | tf_op | source)
XLA Modules:
  0.0 1202.5 jit_solution(4138491207090187145)
XLA Ops:
  6.5 0.0 copy-start
  6.5 0.0 all-gather.3.cloned.1.call-start
  6.5 0.7 all-gather.3.cloned.1.call-update
  7.3 0.0 all-reduce.2.cloned.1.call-start
  7.3 163.5 %all-gather.3.cloned.1.call-done = bf16[4096,512]{1,0:T(8,128)(2,1)} async-done(((bf16[64,512]{1,0:T(8,128)(2,1)}), bf16[4096,512]{1,0:T(8,128)(2,1)}) %all-gather.3.cloned.1.call-update) | async-done | bytes 4194320 | tf_op jit(solution)/shard_map/all_gather | solution.py:11
  170.8 3.2 convolution_convert_fusion
  174.0 13.9 %all_gather.10 = bf16[768,512]{1,0:T(8,128)(2,1)S(1)} all-gather(bf16[96,512]{1,0:T(8,128)(2,1)S(1)} %convolution_convert_fusion), channel_id=1, replica_groups=mesh['dp'=64,'tensor'=8] {'tensor'}, dimensions={0}, use_global_device_ids=true | all-gather | bytes 884736 | tf_op jit(solution)/shard_map/all_gather | solution.py:13
  188.0 0.0 copy-done
  188.0 3.5 convolution_multiply_fusion
  191.4 0.0 copy-start.2
  191.4 0.0 copy-start.3
  191.4 0.0 copy-start.1
  191.5 0.0 all-reduce.2.cloned.1.call-update
  191.5 0.0 all-gather.5.cloned.1.call-start
  191.5 850.6 %all-reduce.2.cloned.1.call-done = f32[512,1792]{1,0:T(8,128)} async-done(((f32[512,1792]{1,0:T(8,128)}), f32[512,1792]{1,0:T(8,128)}) %all-reduce.2.cloned.1.call-update) | async-done | bytes 3670032 | tf_op jit(solution)/shard_map/psum | solution.py:18
  1042.1 3.6 multiply_reduce_fusion
  1045.7 11.0 psum.15
  1057.4 0.0 copy-done.2
  1057.5 0.0 copy-done.3
  1057.5 1.5 fusion.5
  1059.0 0.0 all-gather.5.cloned.1.call-update
  1059.0 134.3 %all-gather.5.cloned.1.call-done = bf16[512,1792]{1,0:T(8,128)(2,1)} async-done(((bf16[8,1792]{1,0:T(8,128)(2,1)}), bf16[512,1792]{1,0:T(8,128)(2,1)}) %all-gather.5.cloned.1.call-update) | async-done | bytes 1835024 | tf_op jit(solution)/shard_map/all_gather | solution.py:33
  1193.3 0.0 copy-done.1
  1193.3 2.7 convolution_bitcast_fusion
Async XLA Ops:
  6.5 181.4 %copy-start = (bf16[768,1792]{1,0:T(8,128)(2,1)S(1)}, bf16[768,1792]{1,0:T(8,128)(2,1)}, u32[]{:S(2)}) copy-start(bf16[768,1792]{1,0:T(8,128)(2,1)} %param.6) | copy-start | bytes 8257540
  6.5 164.3 %all-gather.3.cloned.1.call-start = ((), (), s32[]{:S(2)}) async-start(), calls=%async_computation | async-start | bytes 4259840 | tf_op jit(solution)/shard_map/all_gather | solution.py:11
  7.3 1034.9 %all-reduce.2.cloned.1.call-start = ((), (), s32[]{:S(2)}) async-start(), calls=%async_computation.1 | async-start | bytes 7340032 | tf_op jit(solution)/shard_map/psum | solution.py:18
  191.4 866.0 %copy-start.2 = (f32[8,1792]{1,0:T(8,128)S(1)}, f32[8,1792]{1,0:T(8,128)}, u32[]{:S(2)}) copy-start(f32[8,1792]{1,0:T(8,128)} %param.9) | copy-start | bytes 172036
  191.4 866.0 %copy-start.3 = (f32[8,1792]{1,0:T(8,128)S(1)}, f32[8,1792]{1,0:T(8,128)}, u32[]{:S(2)}) copy-start(f32[8,1792]{1,0:T(8,128)} %param.8) | copy-start | bytes 172036
  191.4 1001.8 %copy-start.1 = (bf16[64,512]{1,0:T(8,128)(2,1)S(1)}, bf16[64,512]{1,0:T(8,128)(2,1)}, u32[]{:S(2)}) copy-start(bf16[64,512]{1,0:T(8,128)(2,1)} %param.7) | copy-start | bytes 196612
  191.5 1001.8 %all-gather.5.cloned.1.call-start = ((), (), s32[]{:S(2)}) async-start(), calls=%async_computation.2 | async-start | bytes 1863680 | tf_op jit(solution)/shard_map/all_gather | solution.py:33
Sparse Core Ops, SparseCore 0:
  11.9 158.8 all-gather.2
  191.6 850.5 all-reduce.1
  1059.1 134.1 all-gather.4
where the time goes:
time: 1200 us
  waiting for transfers between devices  1150 us (96%)
  blocking collectives  25 us (2%)
  between operations  13.8 us (1%)
    psum x1, waiting for transfers between devices, local(): summed = lax.psum(product / count, 'dp')  851 us
    all_gather x1, waiting for transfers between devices, local(): lax.all_gather(basis, 'dp', axis=0, tiled=True)  163 us
    all_gather x1, waiting for transfers between devices, local(): lax.all_gather(direction, 'dp', axis=0, tiled=True)  134 us
  transfers between devices with their start and end apart: 3, of which 3 were waited for; matrix products, arithmetic and copies ran while one was open for 0% of the time, Pallas kernels for 0%

commit v1 on v0

v1 whole, which is shorter than its diff:
```python
import functools

import jax
import jax.numpy as jnp
from jax import lax
from jax.experimental import pallas as pl
from jax.experimental.pallas import tpu as pltpu
from jax.sharding import PartitionSpec as P

MESH = pl.DeviceIdType.MESH
NX, NZ, NY = 4, 8, 4
BLK = 8
TOK = 96
FFL = 1792
HALF = FFL // 2
R = 512
RH = R // 2
BROWS = 64
X_ORDER = (0, 1, 3, 2)
Z_ORDER = (0, 1, 7, 2, 6, 3, 5, 4)
ZH = {1: (0, 1, 2, 3), -1: (7, 6, 5, 4)}
XH = {1: (0, 1), -1: (3, 2)}
SIDES = (1, -1)


class Comm:
    def __init__(self, ssem, rsem, coords):
        self.ssem, self.rsem, self.coords = ssem, rsem, coords
        self.n, self.sent, self.ids = 0, [], {}

    def dev(self, yh=None, x=None, z=None, yl=None, c=None):
        own = self.coords
        yh, x, z, yl, c = (o if v is None else v for v, o in zip((yh, x, z, yl, c), own))
        return (yh * 32 + x * 8 + z, yl * 2 + c)

    def slot(self, key):
        if key not in self.ids:
            self.ids[key] = self.n
            self.n += 1
        return self.ids[key]

    def send(self, key, src, dst, dev):
        i = self.slot(key)
        copy = pltpu.make_async_remote_copy(
            src_ref=src, dst_ref=dst, send_sem=self.ssem.at[i], recv_sem=self.rsem.at[i],
            device_id=dev, device_id_type=MESH,
        )
        copy.start()
        self.sent.append(copy)

    def recv(self, key, dst, dev):
        i = self.slot(key)
        pltpu.make_async_remote_copy(
            src_ref=dst, dst_ref=dst, send_sem=self.ssem.at[i], recv_sem=self.rsem.at[i],
            device_id=dev, device_id_type=MESH,
        ).wait_recv()

    def finish(self):
        for copy in self.sent:
            copy.wait_send()
        self.sent = []


def wrap(v, n):
    return lax.rem(v + n, n)


def gather(comm, name, view_a, view_b, start_b):
    _, x, z, _, _ = comm.coords
    for j in range(1, NX):
        comm.send((name, "ax", j), view_a(x, z), view_a(x, z), comm.dev(x=wrap(x + j, NX)))

    def ring_a(s):
        for j in X_ORDER:
            xo = wrap(x - j, NX)
            if s == 1 and j:
                comm.recv((name, "ax", j), view_a(xo, z), comm.dev())
            for side in SIDES:
                zo = wrap(z - side * (s - 1), NZ)
                if s > 1 and (s < 5 or j in XH[side]):
                    comm.recv((name, "az", side, s - 1, j), view_a(xo, zo), comm.dev())
                if s < 4 or (s == 4 and j in XH[side]):
                    comm.send(
                        (name, "az", side, s, j), view_a(xo, zo), view_a(xo, zo), comm.dev(z=wrap(z + side, NZ))
                    )

    def ring_b1(ks):
        for k in ks:
            zo = wrap(z - k, NZ)
            if k:
                comm.recv((name, "bz", k), view_b(x, zo), comm.dev())
            for side in SIDES:
                comm.send((name, "bx", side, 1, k), view_b(x, zo), view_b(x, zo), comm.dev(x=wrap(x + side, NX)))

    def ring_b2(ks):
        for k in ks:
            zo = wrap(z - k, NZ)
            for side in SIDES:
                xo = wrap(x - side, NX)
                comm.recv((name, "bx", side, 1, k), view_b(xo, zo), comm.dev())
                if k in ZH[side]:
                    comm.send(
                        (name, "bx", side, 2, k), view_b(xo, zo), view_b(xo, zo), comm.dev(x=wrap(x + side, NX))
                    )

    start_b()
    for k in Z_ORDER[1:]:
        comm.send((name, "bz", k), view_b(x, z), view_b(x, z), comm.dev(z=wrap(z + k, NZ)))
    ring_a(1)
    ring_b1(Z_ORDER[:3])
    ring_a(2)
    ring_b1(Z_ORDER[3:])
    ring_b2(Z_ORDER[:3])
    ring_a(3)
    ring_b2(Z_ORDER[3:])
    ring_a(4)
    for side in SIDES:
        for k in ZH[side]:
            comm.recv((name, "bx", side, 2, k), view_b(wrap(x - 2 * side, NX), wrap(z - k, NZ)), comm.dev())
    ring_a(5)


def reduce_scatter(comm, block, sa, ra, sb, rb, sax, rax, sbz, rbz):
    _, x, z, _, _ = comm.coords

    def col(side):
        return 0 if side == 1 else 1

    def xa(j):
        return wrap(x + j, NX)

    def zb(k):
        return wrap(z + k, NZ)

    def step_a(s, js, side):
        for j in js:
            value = block(0, xa(j), wrap(z + side * (4 - s), NZ))
            if s >= 2 or (s == 1 and j in XH[side]):
                got = ra.at[col(side), s - 1, j]
                comm.recv(("ra", side, s - 1, j), got, comm.dev())
                value = value + got[...].astype(jnp.float32)
            out = sa.at[col(side), s, j]
            out[...] = value.astype(jnp.bfloat16)
            comm.send(("ra", side, s, j), out, ra.at[col(side), s, j], comm.dev(z=wrap(z + side, NZ)))

    def step_b(s, ks, side):
        for k in ks:
            value = block(1, wrap(x + side * (2 - s), NX), zb(k))
            if s == 1 and k in ZH[side]:
                got = rb.at[col(side), 0, k]
                comm.recv(("rb", side, 0, k), got, comm.dev())
                value = value + got[...].astype(jnp.float32)
            out = sb.at[col(side), s, k]
            out[...] = value.astype(jnp.bfloat16)
            comm.send(("rb", side, s, k), out, rb.at[col(side), s, k], comm.dev(x=wrap(x + side, NX)))

    def last_b(ks):
        for k in ks:
            value = block(1, x, zb(k))
            for side in SIDES:
                got = rb.at[col(side), 1, k]
                comm.recv(("rb", side, 1, k), got, comm.dev())
                value = value + got[...].astype(jnp.float32)
            if k == 0:
                return value
            sbz[k] = value.astype(jnp.bfloat16)
            comm.send(("rbz", k), sbz.at[k], rbz.at[k], comm.dev(z=zb(k)))

    def last_a(js):
        for j in js:
            value = block(0, xa(j), z)
            for side in SIDES:
                got = ra.at[col(side), 3, j]
                comm.recv(("ra", side, 3, j), got, comm.dev())
                value = value + got[...].astype(jnp.float32)
            if j == 0:
                return value
            sax[j] = value.astype(jnp.bfloat16)
            comm.send(("rax", j), sax.at[j], rax.at[j], comm.dev(x=xa(j)))

    for side in SIDES:
        step_a(0, XH[side], side)
        step_b(0, ZH[side][:2], side)
    for side in SIDES:
        step_a(1, XH[-side], side)
        step_b(0, ZH[side][2:], side)
    for i in (0, 1):
        for side in SIDES:
            step_a(1, XH[side][i:i + 1], side)
            step_b(1, ZH[-side][2 * i:2 * i + 2], side)
    for side in SIDES:
        step_a(2, XH[-side], side)
        step_b(1, ZH[side][:2], side)
    for side in SIDES:
        step_a(2, XH[side], side)
        step_b(1, ZH[side][2:], side)
    for side in SIDES:
        step_a(3, XH[-side], side)
    last_b((4, 3, 5))
    for side in SIDES:
        step_a(3, XH[side], side)
    last_b((2, 6, 1, 7))
    last_a((2, 1, 3))
    total_a = last_a((0,))
    total_b = last_b((0,))
    for j in range(1, NX):
        comm.recv(("rax", j), rax.at[j], comm.dev())
        total_a = total_a + rax[j].astype(jnp.float32)
    for k in range(1, NZ):
        comm.recv(("rbz", k), rbz.at[k], comm.dev())
        total_b = total_b + rbz[k].astype(jnp.float32)
    return total_a, total_b


def kernel(
    tok_ref, up_ref, basis_ref, m_ref, v_ref, out_ref,
    toks, upv, bfull, pall, pt, grad, mom, bp,
    sa, ra, sb, rb, sax, rax, sbz, rbz, ys, yr, n1, n2, da, db,
    lsem, ssem, rsem,
):
    d, t = lax.axis_index("dp"), lax.axis_index("tensor")
    yh, x, z, yl, c = lax.div(d, 32), lax.rem(lax.div(d, 8), 4), lax.rem(d, 8), lax.div(t, 2), lax.rem(t, 2)
    comm = Comm(ssem, rsem, (yh, x, z, yl, c))
    other_core = comm.dev(c=1 - c)
    other_run = comm.dev(yh=1 - yh)
    mirror = comm.dev(yh=1 - yh, yl=3 - yl)

    row0 = pl.multiple_of(yh * BLK, BLK)
    up_copy = pltpu.make_async_copy(up_ref, upv, lsem.at[0])
    tok_copy = pltpu.make_async_copy(tok_ref, toks.at[c], lsem.at[1])
    m_copy = pltpu.make_async_copy(m_ref, mom.at[0, pl.ds(row0, BLK)], lsem.at[2])
    v_copy = pltpu.make_async_copy(v_ref, mom.at[1, pl.ds(row0, BLK)], lsem.at[3])
    for copy in (tok_copy, up_copy, m_copy, v_copy):
        copy.start()

    barrier = pltpu.get_barrier_semaphore()
    peers = [other_core, other_run, mirror]
    peers += [comm.dev(x=wrap(x + j, NX)) for j in range(1, NX)]
    peers += [comm.dev(z=wrap(z + k, NZ)) for k in range(1, NZ)]
    peers += [comm.dev(yl=wrap(yl + r, NY)) for r in range(1, NY)]
    for peer in peers:
        pl.semaphore_signal(barrier, inc=1, device_id=peer, device_id_type=MESH)
    bfull[yh, x, z] = basis_ref[:, pl.ds(pl.multiple_of(c * RH, RH), RH)]
    pl.semaphore_wait(barrier, len(peers))

    comm.send("mirror", bfull.at[yh, x, z], bfull.at[yh, x, z], mirror)

    def start_b():
        comm.send("tok", tok_ref, toks.at[c], other_core)
        comm.send("m", m_ref, mom.at[0, pl.ds(row0, BLK)], other_run)
        comm.send("v", v_ref, mom.at[1, pl.ds(row0, BLK)], other_run)
        row = lax.broadcasted_iota(jnp.int32, (R, R), 0)
        column = lax.broadcasted_iota(jnp.int32, (R, R), 1)
        source = ((column >> 3) & 1) * RH + (column >> 4) * BLK + (column & 7)
        pick = jnp.where(row == source, 1.0, 0.0).astype(jnp.bfloat16)
        bp[...] = jnp.dot(basis_ref[...], pick, preferred_element_type=jnp.float32).astype(jnp.bfloat16)
        comm.recv("mirror", bfull.at[1 - yh, x, z], comm.dev())

    gather(
        comm, "basis",
        lambda xo, zo: bfull.at[yh, xo, zo],
        lambda xo, zo: bfull.at[1 - yh, xo, zo],
        start_b,
    )
    tok_copy.wait()
    comm.recv("tok", toks.at[1 - c], comm.dev())

    proj = jnp.zeros((2 * TOK, RH), jnp.float32)
    depth = NZ * BROWS
    for a in range(2):
        for b in range(NX):
            left = toks[:, :, pl.ds((a * NX + b) * depth, depth)].reshape(2 * TOK, depth)
            proj += jnp.dot(left, bfull[a, b].reshape(depth, RH), preferred_element_type=jnp.float32)
    pall[c, yl] = proj.astype(jnp.bfloat16)

    for r in (2, 1, 3):
        comm.send(("p", r), pall.at[c, yl], pall.at[c, yl], comm.dev(yl=wrap(yl + r, NY)))
    comm.send(("q", 0), pall.at[c, yl], pall.at[c, yl], other_core)
    for r in (1, 3, 2):
        piece = pall.at[c, wrap(yl - r, NY)]
        comm.recv(("p", r), piece, comm.dev())
        comm.send(("q", r), piece, piece, other_core)
    up_copy.wait()

    def product(half):
        pt[...] = pall[half].reshape(NY * 2 * TOK, RH).T

        def tile(i, carry):
            columns = pl.ds(pl.multiple_of(i * 256, 256), 256)
            grad[half, :, columns] = jnp.dot(pt[...], upv[:, columns], preferred_element_type=jnp.float32)
            return carry

        lax.fori_loop(0, FFL // 256, tile, 0)

    product(c)
    for r in range(NY):
        comm.recv(("q", r), pall.at[1 - c, wrap(yl - r, NY)], comm.dev())
    product(1 - c)

    def block(half, xo, zo):
        rows = pl.ds(pl.multiple_of((xo * NZ + zo) * BLK, BLK), BLK)
        columns = pl.ds(half * HALF, HALF)
        return jnp.concatenate([grad[0, rows, columns], grad[1, rows, columns]], axis=0)

    total_a, total_b = reduce_scatter(comm, block, sa, ra, sb, rb, sax, rax, sbz, rbz)
    mine = jnp.concatenate([total_a, total_b], axis=1)
    ys[...] = mine.astype(jnp.bfloat16)
    comm.send("yh", ys, yr, other_run)
    comm.recv("yh", yr, comm.dev())
    g = (mine + yr[...].astype(jnp.float32)) * (1.0 / (NY * 2 * TOK * 64))

    sq = jnp.sum(g * g, axis=0, keepdims=True)
    part = sq[:, 0:128]
    for i in range(1, FFL // 128):
        part = part + sq[:, i * 128:(i + 1) * 128]
    n1[0] = part
    for j in range(NX):
        for k in range(NZ):
            if j or k:
                comm.send(
                    ("n1", j, k), n1.at[0], n1.at[j * NZ + k],
                    comm.dev(x=wrap(x + j, NX), z=wrap(z + k, NZ)),
                )
    for j in range(NX):
        for k in range(NZ):
            if j or k:
                comm.recv(("n1", j, k), n1.at[j * NZ + k], comm.dev())
    n2[0] = jnp.sum(n1[...], axis=0)
    for r in range(NY):
        for e in range(2):
            if r or e:
                comm.send(
                    ("n2", r, e), n2.at[0], n2.at[r * 2 + e],
                    comm.dev(yl=wrap(yl + r, NY), c=lax.rem(c + e, 2)),
                )
    m_copy.wait()
    v_copy.wait()
    other_row0 = pl.multiple_of((1 - yh) * BLK, BLK)
    comm.recv("m", mom.at[0, pl.ds(other_row0, BLK)], comm.dev())
    comm.recv("v", mom.at[1, pl.ds(other_row0, BLK)], comm.dev())
    for r in range(NY):
        for e in range(2):
            if r or e:
                comm.recv(("n2", r, e), n2.at[r * 2 + e], comm.dev())
    norm = jnp.sqrt(jnp.sum(jnp.sum(n2[...], axis=0), axis=1, keepdims=True))
    clipped = g * jnp.minimum(1.0, 1.0 / norm)
    new_first = 0.9 * mom[0] + 0.1 * clipped
    new_second = 0.999 * mom[1] + 0.001 * clipped * clipped
    first_fix = 1.0 - 0.9**20
    second_fix = 1.0 - 0.999**20
    direction = (new_first / first_fix / (jnp.sqrt(new_second / second_fix) + 1e-08)).astype(jnp.bfloat16)
    da[x, z] = direction[:, :HALF]
    db[x, z] = direction[:, HALF:]

    gather(
        comm, "direction",
        lambda xo, zo: da.at[xo, zo],
        lambda xo, zo: db.at[xo, zo],
        lambda: None,
    )
    for half, full in enumerate((da, db)):
        out_ref[:, pl.ds(half * HALF, HALF)] = jnp.dot(
            bp[...], full[...].reshape(R, HALF), preferred_element_type=jnp.float32
        )
    comm.finish()


NSEM = 272


def local(tokens, up_cotangent, basis, first_moment, second_moment):
    bf, f32 = jnp.bfloat16, jnp.float32
    any_spec = pl.BlockSpec(memory_space=pl.ANY)
    vmem_spec = pl.BlockSpec(memory_space=pltpu.VMEM)
    return pl.pallas_call(
        kernel,
        out_shape=jax.ShapeDtypeStruct((BROWS, FFL), f32),
        in_specs=[any_spec, any_spec, vmem_spec, any_spec, any_spec],
        out_specs=vmem_spec,
        scratch_shapes=[
            pltpu.VMEM((2, TOK, 4096), bf),
            pltpu.VMEM((NY * 2 * TOK, FFL), bf),
            pltpu.VMEM((2, NX, NZ, BROWS, RH), bf),
            pltpu.VMEM((2, NY, 2 * TOK, RH), bf),
            pltpu.VMEM((RH, NY * 2 * TOK), bf),
            pltpu.VMEM((2, RH, FFL), f32),
            pltpu.VMEM((2, 2 * BLK, FFL), f32),
            pltpu.VMEM((BROWS, R), bf),
            pltpu.VMEM((2, 4, NX, 16, HALF), bf),
            pltpu.VMEM((2, 4, NX, 16, HALF), bf),
            pltpu.VMEM((2, 2, NZ, 16, HALF), bf),
            pltpu.VMEM((2, 2, NZ, 16, HALF), bf),
            pltpu.VMEM((NX, 16, HALF), bf),
            pltpu.VMEM((NX, 16, HALF), bf),
            pltpu.VMEM((NZ, 16, HALF), bf),
            pltpu.VMEM((NZ, 16, HALF), bf),
            pltpu.VMEM((16, FFL), bf),
            pltpu.VMEM((16, FFL), bf),
            pltpu.VMEM((NX * NZ, 1, 128), f32),
            pltpu.VMEM((NY * 2, 1, 128), f32),
            pltpu.VMEM((NX, NZ, 16, HALF), bf),
            pltpu.VMEM((NX, NZ, 16, HALF), bf),
            pltpu.SemaphoreType.DMA((4,)),
            pltpu.SemaphoreType.DMA((NSEM,)),
            pltpu.SemaphoreType.DMA((NSEM,)),
        ],
        compiler_params=pltpu.CompilerParams(
            collective_id=0, has_side_effects=True, vmem_limit_bytes=48 * 2**20
        ),
        cost_estimate=pl.CostEstimate(flops=4 * 10**9, bytes_accessed=2 * 10**7, transcendentals=0),
        name="galore_step",
    )(tokens, up_cotangent, basis, first_moment, second_moment)


def solution(mesh):
    in_specs = (
        P(("dp", "tensor"), None),
        P("dp", "tensor"),
        P("dp", None),
        P("dp", "tensor"),
        P("dp", "tensor"),
    )
    out_specs = P("dp", "tensor")
    return jax.shard_map(local, mesh=mesh, in_specs=in_specs, out_specs=out_specs, check_vma=False)
```

time: 1200 us -> 122 us (0.10)
  waiting for transfers between devices: 1150 us -> 0 us
  Pallas kernels: 0 us -> 116 us
  blocking collectives: 25 us -> 0 us
  between operations: 13.8 us -> 0.01 us
    psum x1 -> x0, waiting for transfers between devices: 851 us -> none  [local(): summed = lax.psum(product / count, 'dp')]
    all_gather x2 -> x0, waiting for transfers between devices: 298 us -> none  [the longest x1 163 us: local(): lax.all_gather(basis, 'dp', axis=0, tiled=True)]
    pallas_call x0 -> x1, Pallas kernels: none -> 116 us  [local(): pl.pallas_call(kernel, out_shape=jax.ShapeDtypeStruct((BROWS, FFL), f32),...]
    all_gather x1 -> x0, blocking collectives: 13.9 us -> none  [local(): replica = lax.all_gather(projected, 'tensor', axis=0, tiled=True)]
  transfers between devices with their start and end apart: 3 -> 0, of which waited for: 3 -> 0; matrix products, arithmetic and copies ran while one was open for 0% -> 0% of each run, Pallas kernels for 0% -> 0%
where the time goes in v1:
time: 122 us
  Pallas kernels  116 us (95%)
  local copies, waits for them, and re-layouts  6.16 us (5%)
    pallas_call x1, Pallas kernels, local(): pl.pallas_call(kernel, out_shape=jax.ShapeDtypeStruct((BROWS, FFL), f32),...  116 us
    unnamed x11, local copies, waits for them, and re-layouts  6.16 us

profile of v1, /device:TPU:8, one launch (start us, length us, event | category | flops | bytes accessed | tf_op | source)
XLA Modules:
  0.0 121.7 jit_solution(14835721189553164132)
XLA Ops:
  0.0 0.0 copy-start
  0.0 1.8 %copy-done = bf16[768,1792]{1,0:T(8,128)(2,1)S(1)} copy-done((bf16[768,1792]{1,0:T(8,128)(2,1)S(1)}, bf16[768,1792]{1,0:T(8,128)(2,1)}, u32[]{:S(2)}) %copy-start) | copy-done | bytes 2752536
  1.8 0.0 copy-start.1
  1.8 1.1 copy-done.1
  2.9 0.0 copy-start.2
  2.9 0.8 copy-done.2
  3.8 0.0 copy-start.3
  3.8 0.8 copy-done.3
  4.6 0.0 copy-start.4
  4.6 0.8 copy-done.4
  5.4 115.6 %galore_step.1 = f32[64,1792]{1,0:T(8,128)S(1)} custom-call(bf16[96,4096]{1,0:T(8,128)(2,1)S(1)} %copy-done.1, bf16[768,1792]{1,0:T(8,128)(2,1)S(1)} %copy-done, bf16[64,512]{1,0:T(8,128)(2,1)S(1)} %copy-done.2, f32[8,1792]{1,0:T(8,128)S(1)} %copy-done.3, f32[8,1792]{1,0:T(8,128)S(1)} %copy-done.4), custom_call_target="tpu_custom_call" | custom-call | flops 4000000000 | bytes 20000000 | tf_op jit(solution)/shard_map/galore_step/pallas_call | solution.py:375
  121.0 0.8 copy.7
Async XLA Ops:
  0.0 1.8 %copy-start = (bf16[768,1792]{1,0:T(8,128)(2,1)S(1)}, bf16[768,1792]{1,0:T(8,128)(2,1)}, u32[]{:S(2)}) copy-start(bf16[768,1792]{1,0:T(8,128)(2,1)} %up_ref.1) | copy-start | bytes 8257540
  1.8 1.1 copy-start.1
  2.9 0.8 copy-start.2
  3.8 0.8 copy-start.3
  4.6 0.8 copy-start.4

commit v2 on v1

v2 whole, which is shorter than its diff:
```python
import functools

import jax
import jax.numpy as jnp
from jax import lax
from jax.experimental import pallas as pl
from jax.experimental.pallas import tpu as pltpu
from jax.sharding import PartitionSpec as P

MESH = pl.DeviceIdType.MESH
NX, NZ, NY = 4, 8, 4
BLK = 8
TOK = 96
FFL = 1792
WA, WB = 768, 1024
R = 512
RH = R // 2
RQ = RH // 2
BROWS = 64
X_ORDER = (0, 1, 3, 2)
Z_ORDER = (0, 1, -1, 2, -2, 3, -3, 4)
ZH = {1: (0, 1, 2, 3), -1: (-1, -2, -3, 4)}
XH = {1: (0, 1), -1: (3, 2)}
RZH = {1: (3, 1, 2, 0), -1: (4, -3, -1, -2)}
RXH = {1: (0, 2), -1: (1, 3)}
SIDES = (1, -1)


class Comm:
    def __init__(self, ssem, rsem, coords):
        self.ssem, self.rsem, self.coords = ssem, rsem, coords
        self.n, self.sent, self.ids = 0, [], {}

    def dev(self, yh=None, x=None, z=None, yl=None, c=None):
        own = self.coords
        yh, x, z, yl, c = (o if v is None else v for v, o in zip((yh, x, z, yl, c), own))
        return (yh * 32 + x * 8 + z, yl * 2 + c)

    def slot(self, key):
        if key not in self.ids:
            self.ids[key] = self.n
            self.n += 1
        return self.ids[key]

    def send(self, key, src, dst, dev):
        i = self.slot(key)
        copy = pltpu.make_async_remote_copy(
            src_ref=src, dst_ref=dst, send_sem=self.ssem.at[i], recv_sem=self.rsem.at[i],
            device_id=dev, device_id_type=MESH,
        )
        copy.start()
        self.sent.append(copy)

    def recv(self, key, dst, dev):
        i = self.slot(key)
        pltpu.make_async_remote_copy(
            src_ref=dst, dst_ref=dst, send_sem=self.ssem.at[i], recv_sem=self.rsem.at[i],
            device_id=dev, device_id_type=MESH,
        ).wait_recv()

    def finish(self):
        for copy in self.sent:
            copy.wait_send()
        self.sent = []


def wrap(v, n):
    return lax.rem(v + n, n)


def gather(comm, name, view_a, view_b, start_b):
    _, x, z, _, c = comm.coords
    turn = 1 - 2 * c

    def zs(k):
        return wrap(z + turn * k, NZ)

    def ring_a(s, js):
        for j in js:
            xo = wrap(x - j, NX)
            if s == 1 and j:
                comm.recv((name, "ax", j), view_a(xo, z), comm.dev())
            for side in SIDES:
                zo = wrap(z - side * (s - 1), NZ)
                if s > 1 and (s < 5 or j in XH[side]):
                    comm.recv((name, "az", side, s - 1, j), view_a(xo, zo), comm.dev())
                if s < 4 or (s == 4 and j in XH[side]):
                    comm.send(
                        (name, "az", side, s, j), view_a(xo, zo), view_a(xo, zo), comm.dev(z=wrap(z + side, NZ))
                    )

    def send_b(k, origin, hop):
        comm.send((name, "bz", k), view_b(x, origin), view_b(x, origin), comm.dev(z=zs(hop)))

    def ring_b1(ks):
        for k in ks:
            zo = zs(-k)
            if k:
                comm.recv((name, "bz", k), view_b(x, zo), comm.dev())
            if k == 2:
                send_b(3, zo, 1)
                send_b(4, zo, 2)
            if k == -2:
                send_b(-3, zo, -1)
            for side in SIDES:
                comm.send((name, "bx", side, 1, k), view_b(x, zo), view_b(x, zo), comm.dev(x=wrap(x + side, NX)))

    def ring_b2(ks):
        for k in ks:
            zo = zs(-k)
            for side in SIDES:
                xo = wrap(x - side, NX)
                comm.recv((name, "bx", side, 1, k), view_b(xo, zo), comm.dev())
                if k in ZH[side]:
                    comm.send(
                        (name, "bx", side, 2, k), view_b(xo, zo), view_b(xo, zo), comm.dev(x=wrap(x + side, NX))
                    )

    for j in X_ORDER[1:]:
        comm.send((name, "ax", j), view_a(x, z), view_a(x, z), comm.dev(x=wrap(x + j, NX)))
    ring_a(1, X_ORDER[:1])
    start_b()
    for k in (2, -2, 1, -1):
        send_b(k, z, k)
    ring_b1((0,))
    ring_a(1, X_ORDER[1:])
    ring_a(2, X_ORDER[:1])
    ring_b1((1, -1, 2, -2))
    ring_a(2, X_ORDER[1:])
    ring_b2((0,))
    ring_a(3, X_ORDER[:2])
    ring_b1((3, -3, 4))
    ring_b2((1, -1))
    ring_a(3, X_ORDER[2:])
    ring_b2((2, -2))
    ring_a(4, X_ORDER[:2])
    ring_b2((3, -3))
    ring_a(4, X_ORDER[2:])
    ring_b2((4,))
    ring_a(5, X_ORDER)
    for side in SIDES:
        for k in ZH[side]:
            comm.recv((name, "bx", side, 2, k), view_b(wrap(x - 2 * side, NX), zs(-k)), comm.dev())


class Scatter:
    def __init__(self, comm, block, sa, ra, sb, rb, asum, sax, rax, sbz, rbz):
        self.comm, self.block = comm, block
        self.sa, self.ra, self.sb, self.rb = sa, ra, sb, rb
        self.asum, self.sax, self.rax, self.sbz, self.rbz = asum, sax, rax, sbz, rbz
        _, self.x, self.z, _, c = comm.coords
        self.turn = 1 - 2 * c

    def zs(self, k):
        return wrap(self.z + self.turn * k, NZ)

    def step_a(self, s, js, side):
        comm, n = self.comm, 0 if side == 1 else 1
        for j in js:
            value = self.block(0, j, wrap(self.z + side * (4 - s), NZ))
            if s >= 2 or (s == 1 and j in RXH[side]):
                got = self.ra.at[n, s - 1, j]
                comm.recv(("ra", side, s - 1, j), got, comm.dev())
                value = value + got[...].astype(jnp.float32)
            out = self.sa.at[n, s, j]
            out[...] = value.astype(jnp.bfloat16)
            comm.send(("ra", side, s, j), out, self.ra.at[n, s, j], comm.dev(z=wrap(self.z + side, NZ)))

    def step_b(self, s, ks, side):
        comm, n = self.comm, 0 if side == 1 else 1
        for k in ks:
            value = self.block(1, wrap(self.x + side * (2 - s), NX), self.zs(k))
            if s == 1 and k in RZH[side]:
                got = self.rb.at[n, 0, k % NZ]
                comm.recv(("rb", side, 0, k), got, comm.dev())
                value = value + got[...].astype(jnp.float32)
            out = self.sb.at[n, s, k % NZ]
            out[...] = value.astype(jnp.bfloat16)
            comm.send(("rb", side, s, k), out, self.rb.at[n, s, k % NZ], comm.dev(x=wrap(self.x + side, NX)))

    def last_a(self, js):
        comm = self.comm
        for j in js:
            value = self.block(0, j, self.z)
            for n, side in enumerate(SIDES):
                got = self.ra.at[n, 3, j]
                comm.recv(("ra", side, 3, j), got, comm.dev())
                value = value + got[...].astype(jnp.float32)
            self.asum[j] = value
            self.sax[j] = value.astype(jnp.bfloat16)

    def send_a(self):
        for j in (2, 1, 3):
            xo = wrap(self.x + j, NX)
            self.comm.send(("rax", j), self.sax.at[xo], self.rax.at[j], self.comm.dev(x=xo))

    def total_a(self):
        value = self.asum[self.x]
        for j in (1, 3, 2):
            self.comm.recv(("rax", j), self.rax.at[j], self.comm.dev())
            value = value + self.rax[j].astype(jnp.float32)
        return value

    def got_b(self, k):
        self.comm.recv(("rbz", k), self.rbz.at[k % NZ], self.comm.dev())
        return self.rbz[k % NZ].astype(jnp.float32)

    def last_b(self, ks):
        comm = self.comm
        hop = {3: 1, -3: -1, 4: 2}
        for k in ks:
            value = self.block(1, self.x, self.zs(k))
            for n, side in enumerate(SIDES):
                got = self.rb.at[n, 1, k % NZ]
                comm.recv(("rb", side, 1, k), got, comm.dev())
                value = value + got[...].astype(jnp.float32)
            if k == 2:
                value = value + self.got_b(3) + self.got_b(4)
            if k == -2:
                value = value + self.got_b(-3)
            if k == 0:
                for other in (1, -1, 2, -2):
                    value = value + self.got_b(other)
                return value
            self.sbz[k % NZ] = value.astype(jnp.bfloat16)
            comm.send(("rbz", k), self.sbz.at[k % NZ], self.rbz.at[k % NZ], comm.dev(z=self.zs(hop.get(k, k))))

    def early(self, js):
        for side in SIDES:
            self.step_a(0, [j for j in js if j in RXH[side]], side)
        for side in SIDES:
            self.step_a(1, [j for j in js if j not in RXH[side]], side)

    def rest(self):
        def a(s, js):
            for side in SIDES:
                self.step_a(s, js[side], side)

        first = {1: (0,), -1: (1,)}
        cross = {1: (1,), -1: (0,)}
        first2 = {1: (2,), -1: (3,)}
        cross2 = {1: (3,), -1: (2,)}
        for side in SIDES:
            self.step_b(0, RZH[side][:2], side)
        a(1, first)
        self.early((2, 3))
        for side in SIDES:
            self.step_b(0, RZH[side][2:], side)
        a(2, cross)
        for side in SIDES:
            self.step_b(1, RZH[-side], side)
        a(2, first)
        a(1, first2)
        for side in SIDES:
            self.step_b(1, RZH[side][:2], side)
        a(3, cross)
        a(2, cross2)
        a(3, first)
        for side in SIDES:
            self.step_b(1, RZH[side][2:], side)
        a(2, first2)
        self.last_b((4, 3, -3))
        a(3, cross2)
        self.last_b((1, -1))
        a(3, first2)
        self.last_a((0, 1))
        self.last_b((2, -2))
        self.last_a((2, 3))
        self.send_a()
        value_b = self.last_b((0,))
        value_a = self.total_a()
        return value_a, value_b


def kernel(
    tok_ref, up_ref, basis_ref, m_ref, v_ref, out_ref,
    toks, upv, bas, bfull, pall, pt, grad, mom, bp,
    sa, ra, sb, rb, asum, sax, rax, sbz, rbz, ysa, yra, ysb, yrb, n1, n2, da, db,
    lsem, ssem, rsem,
):
    d, t = lax.axis_index("dp"), lax.axis_index("tensor")
    yh, x, z, yl, c = lax.div(d, 32), lax.rem(lax.div(d, 8), 4), lax.rem(d, 8), lax.div(t, 2), lax.rem(t, 2)
    comm = Comm(ssem, rsem, (yh, x, z, yl, c))
    other_core = comm.dev(c=1 - c)
    other_run = comm.dev(yh=1 - yh)
    mirror = comm.dev(yh=1 - yh, yl=3 - yl)

    half_columns = pl.ds(pl.multiple_of(c * RH, RH), RH)
    b_copy = pltpu.make_async_copy(basis_ref.at[:, half_columns], bfull.at[yh, x, z], lsem.at[0])
    b_copy.start()
    barrier = pltpu.get_barrier_semaphore()
    peers = [other_core, other_run, mirror]
    peers += [comm.dev(x=wrap(x + j, NX)) for j in range(1, NX)]
    peers += [comm.dev(z=wrap(z + k, NZ)) for k in range(1, NZ)]
    peers += [comm.dev(yl=wrap(yl + r, NY)) for r in range(1, NY)]
    for peer in peers:
        pl.semaphore_signal(barrier, inc=1, device_id=peer, device_id_type=MESH)

    row0 = pl.multiple_of(yh * BLK, BLK)
    tok_copy = pltpu.make_async_copy(tok_ref, toks.at[c], lsem.at[1])
    up_copy = pltpu.make_async_copy(up_ref, upv, lsem.at[2])
    m_copy = pltpu.make_async_copy(m_ref, mom.at[0, pl.ds(row0, BLK)], lsem.at[3])
    v_copy = pltpu.make_async_copy(v_ref, mom.at[1, pl.ds(row0, BLK)], lsem.at[4])
    bas_copy = pltpu.make_async_copy(basis_ref, bas, lsem.at[5])
    for copy in (tok_copy, up_copy, m_copy, v_copy, bas_copy):
        copy.start()
    b_copy.wait()
    pl.semaphore_wait(barrier, len(peers))

    comm.send("mirror", bfull.at[yh, x, z], bfull.at[yh, x, z], mirror)

    def start_b():
        comm.send("tok", tok_ref, toks.at[c], other_core)
        comm.send("m", m_ref, mom.at[0, pl.ds(row0, BLK)], other_run)
        comm.send("v", v_ref, mom.at[1, pl.ds(row0, BLK)], other_run)
        comm.recv("mirror", bfull.at[1 - yh, x, z], comm.dev())

    gather(
        comm, "basis",
        lambda xo, zo: bfull.at[yh, xo, zo],
        lambda xo, zo: bfull.at[1 - yh, xo, zo],
        start_b,
    )
    tok_copy.wait()
    comm.recv("tok", toks.at[1 - c], comm.dev())

    proj = jnp.zeros((2 * TOK, RH), jnp.float32)
    depth = NZ * BROWS
    for a in range(2):
        for b in range(NX):
            left = toks[:, :, pl.ds((a * NX + b) * depth, depth)].reshape(2 * TOK, depth)
            proj += jnp.dot(left, bfull[a, b].reshape(depth, RH), preferred_element_type=jnp.float32)
    proj = proj.astype(jnp.bfloat16)

    for q in range(2):
        piece = pall.at[c, q, yl]
        piece[...] = proj[:, q * RQ:(q + 1) * RQ]
        for r in (2, 1, 3):
            comm.send(("p", q, r), piece, piece, comm.dev(yl=wrap(yl + r, NY)))
        comm.send(("q", q, 0), piece, piece, other_core)

    def collect(q):
        for r in (1, 3, 2):
            piece = pall.at[c, q, wrap(yl - r, NY)]
            comm.recv(("p", q, r), piece, comm.dev())
            comm.send(("q", q, r), piece, piece, other_core)
        for r in (0, 1, 3, 2):
            comm.recv(("q", q, r), pall.at[1 - c, q, wrap(yl - r, NY)], comm.dev())

    def product(q):
        for half in range(2):
            pt[half] = pall[half, q].reshape(NY * 2 * TOK, RQ).T

        def tile(i, carry):
            columns = pl.ds(pl.multiple_of(i * 256, 256), 256)
            left = pt[...].reshape(2 * RQ, NY * 2 * TOK)
            value = jnp.dot(left, upv[:, columns], preferred_element_type=jnp.float32)
            for half in range(2):
                grad[half, pl.ds(q * RQ, RQ), columns] = value[half * RQ:(half + 1) * RQ]
            return carry

        lax.fori_loop(0, FFL // 256, tile, 0)

    def block(half, xo, zo):
        rows = pl.ds(pl.multiple_of((xo * NZ + zo) * BLK, BLK), BLK)
        columns = pl.ds(half * WA, WB if half else WA)
        return jnp.concatenate([grad[0, rows, columns], grad[1, rows, columns]], axis=0)

    scatter = Scatter(comm, block, sa, ra, sb, rb, asum, sax, rax, sbz, rbz)
    collect(0)
    up_copy.wait()
    product(0)
    scatter.early((0, 1))
    collect(1)
    product(1)
    total_a, total_b = scatter.rest()
    sums = []
    for name, value, ys, yr in (("ya", total_a, ysa, yra), ("yb", total_b, ysb, yrb)):
        ys[...] = value.astype(jnp.bfloat16)
        comm.send(name, ys, yr, other_run)
    for name, value, yr in (("ya", total_a, yra), ("yb", total_b, yrb)):
        comm.recv(name, yr, comm.dev())
        sums.append(value + yr[...].astype(jnp.float32))
    g = jnp.concatenate(sums, axis=1) * (1.0 / (NY * 2 * TOK * 64))

    sq = jnp.sum(g * g, axis=0, keepdims=True)
    part = sq[:, 0:128]
    for i in range(1, FFL // 128):
        part = part + sq[:, i * 128:(i + 1) * 128]
    n1[0] = part
    for j in range(NX):
        for k in range(NZ):
            if j or k:
                comm.send(
                    ("n1", j, k), n1.at[0], n1.at[j * NZ + k],
                    comm.dev(x=wrap(x + j, NX), z=wrap(z + k, NZ)),
                )
    for j in range(NX):
        for k in range(NZ):
            if j or k:
                comm.recv(("n1", j, k), n1.at[j * NZ + k], comm.dev())
    n2[0] = jnp.sum(n1[...], axis=0)
    for r in range(NY):
        for e in range(2):
            if r or e:
                comm.send(
                    ("n2", r, e), n2.at[0], n2.at[r * 2 + e],
                    comm.dev(yl=wrap(yl + r, NY), c=lax.rem(c + e, 2)),
                )
    bas_copy.wait()
    row = lax.broadcasted_iota(jnp.int32, (R, R), 0)
    column = lax.broadcasted_iota(jnp.int32, (R, R), 1)
    source = ((column >> 3) & 1) * RH + (column >> 4) * BLK + (column & 7)
    pick = jnp.where(row == source, 1.0, 0.0).astype(jnp.bfloat16)
    bp[...] = jnp.dot(bas[...], pick, preferred_element_type=jnp.float32).astype(jnp.bfloat16)
    m_copy.wait()
    v_copy.wait()
    other_row0 = pl.multiple_of((1 - yh) * BLK, BLK)
    comm.recv("m", mom.at[0, pl.ds(other_row0, BLK)], comm.dev())
    comm.recv("v", mom.at[1, pl.ds(other_row0, BLK)], comm.dev())
    for r in range(NY):
        for e in range(2):
            if r or e:
                comm.recv(("n2", r, e), n2.at[r * 2 + e], comm.dev())
    norm = jnp.sqrt(jnp.sum(jnp.sum(n2[...], axis=0), axis=1, keepdims=True))
    clipped = g * jnp.minimum(1.0, 1.0 / norm)
    new_first = 0.9 * mom[0] + 0.1 * clipped
    new_second = 0.999 * mom[1] + 0.001 * clipped * clipped
    first_fix = 1.0 - 0.9**20
    second_fix = 1.0 - 0.999**20
    direction = (new_first / first_fix / (jnp.sqrt(new_second / second_fix) + 1e-08)).astype(jnp.bfloat16)
    da[x, z] = direction[:, :WA]
    db[x, z] = direction[:, WA:]

    gather(
        comm, "direction",
        lambda xo, zo: da.at[xo, zo],
        lambda xo, zo: db.at[xo, zo],
        lambda: None,
    )
    for start, full, width in ((0, da, WA), (WA, db, WB)):
        out_ref[:, pl.ds(start, width)] = jnp.dot(
            bp[...], full[...].reshape(R, width), preferred_element_type=jnp.float32
        )
    comm.finish()


NSEM = 272


def local(tokens, up_cotangent, basis, first_moment, second_moment):
    bf, f32 = jnp.bfloat16, jnp.float32
    hbm_spec = pl.BlockSpec(memory_space=pltpu.HBM)
    vmem_spec = pl.BlockSpec(memory_space=pltpu.VMEM)
    return pl.pallas_call(
        kernel,
        out_shape=jax.ShapeDtypeStruct((BROWS, FFL), f32),
        in_specs=[hbm_spec] * 5,
        out_specs=vmem_spec,
        scratch_shapes=[
            pltpu.VMEM((2, TOK, 4096), bf),
            pltpu.VMEM((NY * 2 * TOK, FFL), bf),
            pltpu.VMEM((BROWS, R), bf),
            pltpu.VMEM((2, NX, NZ, BROWS, RH), bf),
            pltpu.VMEM((2, 2, NY, 2 * TOK, RQ), bf),
            pltpu.VMEM((2, RQ, NY * 2 * TOK), bf),
            pltpu.VMEM((2, RH, FFL), f32),
            pltpu.VMEM((2, 2 * BLK, FFL), f32),
            pltpu.VMEM((BROWS, R), bf),
            pltpu.VMEM((2, 4, NX, 16, WA), bf),
            pltpu.VMEM((2, 4, NX, 16, WA), bf),
            pltpu.VMEM((2, 2, NZ, 16, WB), bf),
            pltpu.VMEM((2, 2, NZ, 16, WB), bf),
            pltpu.VMEM((NX, 16, WA), f32),
            pltpu.VMEM((NX, 16, WA), bf),
            pltpu.VMEM((NX, 16, WA), bf),
            pltpu.VMEM((NZ, 16, WB), bf),
            pltpu.VMEM((NZ, 16, WB), bf),
            pltpu.VMEM((16, WA), bf),
            pltpu.VMEM((16, WA), bf),
            pltpu.VMEM((16, WB), bf),
            pltpu.VMEM((16, WB), bf),
            pltpu.VMEM((NX * NZ, 1, 128), f32),
            pltpu.VMEM((NY * 2, 1, 128), f32),
            pltpu.VMEM((NX, NZ, 16, WA), bf),
            pltpu.VMEM((NX, NZ, 16, WB), bf),
            pltpu.SemaphoreType.DMA((6,)),
            pltpu.SemaphoreType.DMA((NSEM,)),
            pltpu.SemaphoreType.DMA((NSEM,)),
        ],
        compiler_params=pltpu.CompilerParams(
            collective_id=0, has_side_effects=True, vmem_limit_bytes=48 * 2**20
        ),
        cost_estimate=pl.CostEstimate(flops=4 * 10**9, bytes_accessed=2 * 10**7, transcendentals=0),
        name="galore_step",
    )(tokens, up_cotangent, basis, first_moment, second_moment)


def solution(mesh):
    in_specs = (
        P(("dp", "tensor"), None),
        P("dp", "tensor"),
        P("dp", None),
        P("dp", "tensor"),
        P("dp", "tensor"),
    )
    out_specs = P("dp", "tensor")
    return jax.shard_map(local, mesh=mesh, in_specs=in_specs, out_specs=out_specs, check_vma=False)
```

time: 122 us -> 115 us (0.943)
  the two profiles are of different devices: /device:TPU:8 before, /device:TPU:4 now
where the time goes in v2:
time: 115 us; the launch traced here: 114 us
  Pallas kernels  108 us (94%)
  local copies, waits for them, and re-layouts  6.16 us (5%)
    pallas_call x1, Pallas kernels, local(): pl.pallas_call(kernel, out_shape=jax.ShapeDtypeStruct((BROWS, FFL), f32),...  108 us
    unnamed x11, local copies, waits for them, and re-layouts  6.16 us

profile of v2, /device:TPU:4, one launch (start us, length us, event | category | flops | bytes accessed | tf_op | source)
XLA Modules:
  0.0 114.3 jit_solution(4856591510761443130)
XLA Ops:
  0.0 0.0 copy-start
  0.0 1.8 %copy-done = bf16[768,1792]{1,0:T(8,128)(2,1)S(1)} copy-done((bf16[768,1792]{1,0:T(8,128)(2,1)S(1)}, bf16[768,1792]{1,0:T(8,128)(2,1)}, u32[]{:S(2)}) %copy-start) | copy-done | bytes 2752536
  1.8 0.0 copy-start.1
  1.8 1.1 copy-done.1
  2.9 0.0 copy-start.2
  2.9 0.8 copy-done.2
  3.8 0.0 copy-start.3
  3.8 0.8 copy-done.3
  4.6 0.0 copy-start.4
  4.6 0.8 copy-done.4
  5.4 108.2 %galore_step.1 = f32[64,1792]{1,0:T(8,128)S(1)} custom-call(bf16[96,4096]{1,0:T(8,128)(2,1)S(1)} %copy-done.1, bf16[768,1792]{1,0:T(8,128)(2,1)S(1)} %copy-done, bf16[64,512]{1,0:T(8,128)(2,1)S(1)} %copy-done.2, f32[8,1792]{1,0:T(8,128)S(1)} %copy-done.3, f32[8,1792]{1,0:T(8,128)S(1)} %copy-done.4), custom_call_target="tpu_custom_call" | custom-call | flops 4000000000 | bytes 20000000 | tf_op jit(solution)/shard_map/galore_step/pallas_call | solution.py:455
  113.6 0.8 copy.7
Async XLA Ops:
  0.0 1.8 %copy-start = (bf16[768,1792]{1,0:T(8,128)(2,1)S(1)}, bf16[768,1792]{1,0:T(8,128)(2,1)}, u32[]{:S(2)}) copy-start(bf16[768,1792]{1,0:T(8,128)(2,1)} %up_ref.1) | copy-start | bytes 8257540
  1.8 1.1 copy-start.1
  2.9 0.8 copy-start.2
  3.8 0.8 copy-start.3
  4.6 0.8 copy-start.4

commit v3 on v2

v3 whole, which is shorter than its diff:
```python
import functools

import jax
import jax.numpy as jnp
from jax import lax
from jax.experimental import pallas as pl
from jax.experimental.pallas import tpu as pltpu
from jax.sharding import PartitionSpec as P

MESH = pl.DeviceIdType.MESH
NX, NZ, NY = 4, 8, 4
BLK = 8
TOK = 96
FFL = 1792
WA, WB = 768, 1024
R = 512
RH = R // 2
RQ = RH // 2
BROWS = 64
X_ORDER = (0, 1, 3, 2)
Z_ORDER = (0, 1, -1, 2, -2, 3, -3, 4)
ZH = {1: (0, 1, 2, 3), -1: (-1, -2, -3, 4)}
XH = {1: (0, 1), -1: (3, 2)}
RZH = {1: (3, 1, 2, 0), -1: (4, -3, -1, -2)}
RXH = {1: (0, 2), -1: (1, 3)}
SIDES = (1, -1)


class Comm:
    def __init__(self, ssem, rsem, coords):
        self.ssem, self.rsem, self.coords = ssem, rsem, coords
        self.n, self.sent, self.ids = 0, [], {}

    def dev(self, yh=None, x=None, z=None, yl=None, c=None):
        own = self.coords
        yh, x, z, yl, c = (o if v is None else v for v, o in zip((yh, x, z, yl, c), own))
        return (yh * 32 + x * 8 + z, yl * 2 + c)

    def slot(self, key):
        if key not in self.ids:
            self.ids[key] = self.n
            self.n += 1
        return self.ids[key]

    def send(self, key, src, dst, dev):
        i = self.slot(key)
        copy = pltpu.make_async_remote_copy(
            src_ref=src, dst_ref=dst, send_sem=self.ssem.at[i], recv_sem=self.rsem.at[i],
            device_id=dev, device_id_type=MESH,
        )
        copy.start()
        self.sent.append(copy)

    def recv(self, key, dst, dev):
        i = self.slot(key)
        pltpu.make_async_remote_copy(
            src_ref=dst, dst_ref=dst, send_sem=self.ssem.at[i], recv_sem=self.rsem.at[i],
            device_id=dev, device_id_type=MESH,
        ).wait_recv()

    def finish(self):
        for copy in self.sent:
            copy.wait_send()
        self.sent = []


def wrap(v, n):
    return lax.rem(v + n, n)


def run(tasks):
    for _, step in sorted(tasks, key=lambda task: task[0]):
        step()


def gather(comm, name, view_a, view_b, begin, begin_b):
    _, x, z, _, c = comm.coords
    turn = 1 - 2 * c

    def zs(k):
        return wrap(z + turn * k, NZ)

    def send_ax():
        for j in X_ORDER[1:]:
            comm.send((name, "ax", j), view_a(x, z), view_a(x, z), comm.dev(x=wrap(x + j, NX)))

    def ring_a(s, js):
        for j in js:
            xo = wrap(x - j, NX)
            if s == 1 and j:
                comm.recv((name, "ax", j), view_a(xo, z), comm.dev())
            for side in SIDES:
                zo = wrap(z - side * (s - 1), NZ)
                if s > 1 and (s < 5 or j in XH[side]):
                    comm.recv((name, "az", side, s - 1, j), view_a(xo, zo), comm.dev())
                if s < 4 or (s == 4 and j in XH[side]):
                    comm.send(
                        (name, "az", side, s, j), view_a(xo, zo), view_a(xo, zo), comm.dev(z=wrap(z + side, NZ))
                    )

    def send_b(k, origin, hop):
        comm.send((name, "bz", k), view_b(x, origin), view_b(x, origin), comm.dev(z=zs(hop)))

    def send_bz():
        for k in (2, -2, 1, -1):
            send_b(k, z, k)

    def ring_b1(ks):
        for k in ks:
            zo = zs(-k)
            if k:
                comm.recv((name, "bz", k), view_b(x, zo), comm.dev())
            if k == 2:
                send_b(3, zo, 1)
                send_b(4, zo, 2)
            if k == -2:
                send_b(-3, zo, -1)
            for side in SIDES:
                comm.send((name, "bx", side, 1, k), view_b(x, zo), view_b(x, zo), comm.dev(x=wrap(x + side, NX)))

    def ring_b2(ks):
        for k in ks:
            zo = zs(-k)
            for side in SIDES:
                xo = wrap(x - side, NX)
                comm.recv((name, "bx", side, 1, k), view_b(xo, zo), comm.dev())
                if k in ZH[side]:
                    comm.send(
                        (name, "bx", side, 2, k), view_b(xo, zo), view_b(xo, zo), comm.dev(x=wrap(x + side, NX))
                    )

    def last_b():
        for side in SIDES:
            for k in ZH[side]:
                comm.recv((name, "bx", side, 2, k), view_b(wrap(x - 2 * side, NX), zs(-k)), comm.dev())

    steps_a = [
        (0.0, send_ax), (0.0, lambda: ring_a(1, (0,))),
        (2.3, lambda: ring_a(2, (0,))), (2.4, lambda: ring_a(1, (1, 3))), (2.9, lambda: ring_a(1, (2,))),
        (4.6, lambda: ring_a(3, (0,))), (4.7, lambda: ring_a(2, (1, 3))), (5.2, lambda: ring_a(2, (2,))),
        (7.0, lambda: ring_a(4, (0,))), (7.2, lambda: ring_a(3, (1, 3))), (7.6, lambda: ring_a(3, (2,))),
        (9.5, lambda: ring_a(4, (1, 3))), (9.9, lambda: ring_a(4, (2,))), (12.3, lambda: ring_a(5, X_ORDER)),
    ]
    steps_b = [
        (0.0, send_bz), (0.0, lambda: ring_b1((0,))),
        (2.3, lambda: ring_b1((1, -1))), (2.4, lambda: ring_b2((0,))), (3.0, lambda: ring_b1((2, -2))),
        (4.7, lambda: ring_b2((1, -1))), (5.4, lambda: ring_b2((2, -2))), (6.0, lambda: ring_b1((3, -3, 4))),
        (8.5, lambda: ring_b2((3, -3, 4))), (10.7, last_b),
    ]
    return [(begin + t, f) for t, f in steps_a] + [(begin_b + t, f) for t, f in steps_b]


class Scatter:
    def __init__(self, comm, name, block, sa, ra, sb, rb, asum, sax, rax, sbz, rbz):
        self.comm, self.name, self.block = comm, name, block
        self.sa, self.ra, self.sb, self.rb = sa, ra, sb, rb
        self.asum, self.sax, self.rax, self.sbz, self.rbz = asum, sax, rax, sbz, rbz
        _, self.x, self.z, _, c = comm.coords
        self.turn = 1 - 2 * c

    def zs(self, k):
        return wrap(self.z + self.turn * k, NZ)

    def step_a(self, s, js, side):
        comm, n = self.comm, 0 if side == 1 else 1
        for j in js:
            value = self.block(0, j, wrap(self.z + side * (4 - s), NZ))
            if s >= 2 or (s == 1 and j in RXH[side]):
                got = self.ra.at[n, s - 1, j]
                comm.recv((self.name, "ra", side, s - 1, j), got, comm.dev())
                value = value + got[...].astype(jnp.float32)
            out = self.sa.at[n, s, j]
            out[...] = value.astype(jnp.bfloat16)
            comm.send((self.name, "ra", side, s, j), out, self.ra.at[n, s, j], comm.dev(z=wrap(self.z + side, NZ)))

    def step_b(self, s, ks, side):
        comm, n = self.comm, 0 if side == 1 else 1
        for k in ks:
            value = self.block(1, wrap(self.x + side * (2 - s), NX), self.zs(k))
            if s == 1 and k in RZH[side]:
                got = self.rb.at[n, 0, k % NZ]
                comm.recv((self.name, "rb", side, 0, k), got, comm.dev())
                value = value + got[...].astype(jnp.float32)
            out = self.sb.at[n, s, k % NZ]
            out[...] = value.astype(jnp.bfloat16)
            comm.send((self.name, "rb", side, s, k), out, self.rb.at[n, s, k % NZ], comm.dev(x=wrap(self.x + side, NX)))

    def last_a(self, js):
        comm = self.comm
        for j in js:
            value = self.block(0, j, self.z)
            for n, side in enumerate(SIDES):
                got = self.ra.at[n, 3, j]
                comm.recv((self.name, "ra", side, 3, j), got, comm.dev())
                value = value + got[...].astype(jnp.float32)
            self.asum[j] = value
            self.sax[j] = value.astype(jnp.bfloat16)

    def send_a(self):
        for j in (2, 1, 3):
            xo = wrap(self.x + j, NX)
            self.comm.send((self.name, "rax", j), self.sax.at[xo], self.rax.at[j], self.comm.dev(x=xo))

    def total_a(self):
        value = self.asum[self.x]
        for j in (1, 3, 2):
            self.comm.recv((self.name, "rax", j), self.rax.at[j], self.comm.dev())
            value = value + self.rax[j].astype(jnp.float32)
        return value

    def got_b(self, k):
        self.comm.recv((self.name, "rbz", k), self.rbz.at[k % NZ], self.comm.dev())
        return self.rbz[k % NZ].astype(jnp.float32)

    def last_b(self, ks):
        comm = self.comm
        hop = {3: 1, -3: -1, 4: 2}
        for k in ks:
            value = self.block(1, self.x, self.zs(k))
            for n, side in enumerate(SIDES):
                got = self.rb.at[n, 1, k % NZ]
                comm.recv((self.name, "rb", side, 1, k), got, comm.dev())
                value = value + got[...].astype(jnp.float32)
            if k == 2:
                value = value + self.got_b(3) + self.got_b(4)
            if k == -2:
                value = value + self.got_b(-3)
            if k == 0:
                for other in (1, -1, 2, -2):
                    value = value + self.got_b(other)
                return value
            self.sbz[k % NZ] = value.astype(jnp.bfloat16)
            comm.send((self.name, "rbz", k), self.sbz.at[k % NZ], self.rbz.at[k % NZ], comm.dev(z=self.zs(hop.get(k, k))))

    def steps(self, begin):
        def a(s, prior):
            for side in SIDES:
                self.step_a(s, RXH[side if prior else -side], side)

        def b(s, prior):
            for side in SIDES:
                self.step_b(s, RZH[side if prior else -side], side)

        steps = [
            (0.0, lambda: a(0, True)), (0.0, lambda: b(0, True)), (0.2, lambda: a(1, False)), (0.3, lambda: b(1, False)),
            (2.3, lambda: a(1, True)), (2.5, lambda: a(2, False)), (2.6, lambda: b(1, True)),
            (4.6, lambda: a(2, True)), (4.9, lambda: a(3, False)),
            (5.2, lambda: self.last_b((4, 3, -3))), (5.8, lambda: self.last_b((1, -1))),
            (7.0, lambda: a(3, True)), (8.5, lambda: self.last_b((2, -2))),
            (9.4, lambda: self.last_a(range(NX))), (9.4, self.send_a),
        ]
        return [(begin + t, f) for t, f in steps]


def kernel(
    tok_ref, up_ref, basis_ref, m_ref, v_ref, out_ref,
    toks, upv, bas, bfull, pall, pt, grad, mom, bp,
    sa, ra, sb, rb, asum, sax, rax, sbz, rbz, ysa, yra, ysb, yrb, gsum, n1, n2, da, db,
    lsem, ssem, rsem,
):
    d, t = lax.axis_index("dp"), lax.axis_index("tensor")
    yh, x, z, yl, c = lax.div(d, 32), lax.rem(lax.div(d, 8), 4), lax.rem(d, 8), lax.div(t, 2), lax.rem(t, 2)
    comm = Comm(ssem, rsem, (yh, x, z, yl, c))
    other_core = comm.dev(c=1 - c)
    other_run = comm.dev(yh=1 - yh)
    mirror = comm.dev(yh=1 - yh, yl=3 - yl)

    b_copies = []
    for q in range(2):
        columns = pl.ds(pl.multiple_of(q * RH + c * RQ, RQ), RQ)
        b_copies.append(pltpu.make_async_copy(basis_ref.at[:, columns], bfull.at[q, yh, x, z], lsem.at[5 + q]))
        b_copies[q].start()
    barrier = pltpu.get_barrier_semaphore()
    peers = [other_core, mirror]
    peers += [comm.dev(x=wrap(x + j, NX)) for j in range(1, NX)]
    peers += [comm.dev(z=wrap(z + k, NZ)) for k in (1, -1, 2, -2)]
    peers += [comm.dev(yl=wrap(yl + r, NY)) for r in range(1, NY)]
    for peer in peers:
        pl.semaphore_signal(barrier, inc=1, device_id=peer, device_id_type=MESH)

    row0 = pl.multiple_of(yh * BLK, BLK)
    tok_copy = pltpu.make_async_copy(tok_ref, toks.at[c], lsem.at[0])
    up_copy = pltpu.make_async_copy(up_ref, upv, lsem.at[1])
    m_copy = pltpu.make_async_copy(m_ref, mom.at[0, pl.ds(row0, BLK)], lsem.at[2])
    v_copy = pltpu.make_async_copy(v_ref, mom.at[1, pl.ds(row0, BLK)], lsem.at[3])
    bas_copy = pltpu.make_async_copy(basis_ref, bas, lsem.at[4])
    for copy in (tok_copy, up_copy, m_copy, v_copy, bas_copy):
        copy.start()
    for copy in b_copies:
        copy.wait()
    pl.semaphore_wait(barrier, len(peers))

    def send_mirror(q):
        comm.send(("mirror", q), bfull.at[q, yh, x, z], bfull.at[q, yh, x, z], mirror)

    def recv_mirror(q):
        comm.recv(("mirror", q), bfull.at[q, 1 - yh, x, z], comm.dev())

    def send_tokens():
        comm.send("tok", tok_ref, toks.at[c], other_core)

    def recv_tokens():
        tok_copy.wait()
        comm.recv("tok", toks.at[1 - c], comm.dev())

    def send_moments():
        comm.send("m", m_ref, mom.at[0, pl.ds(row0, BLK)], other_run)
        comm.send("v", v_ref, mom.at[1, pl.ds(row0, BLK)], other_run)

    def project(q):
        proj = jnp.zeros((2 * TOK, RQ), jnp.float32)
        depth = NZ * BROWS
        for a in range(2):
            for b in range(NX):
                left = toks[:, :, pl.ds((a * NX + b) * depth, depth)].reshape(2 * TOK, depth)
                proj += jnp.dot(left, bfull[q, a, b].reshape(depth, RQ), preferred_element_type=jnp.float32)
        piece = pall.at[q, c, yl]
        piece[...] = proj.astype(jnp.bfloat16)
        for r in (2, 1, 3):
            comm.send(("p", q, r), piece, piece, comm.dev(yl=wrap(yl + r, NY)))
        comm.send(("q", q, 0), piece, piece, other_core)

    def collect(q):
        for r in (1, 3, 2):
            piece = pall.at[q, c, wrap(yl - r, NY)]
            comm.recv(("p", q, r), piece, comm.dev())
            comm.send(("q", q, r), piece, piece, other_core)

    def product(q):
        for r in (0, 1, 3, 2):
            comm.recv(("q", q, r), pall.at[q, 1 - c, wrap(yl - r, NY)], comm.dev())
        for half in range(2):
            pt[half] = pall[q, half].reshape(NY * 2 * TOK, RQ).T

        def tile(i, carry):
            columns = pl.ds(pl.multiple_of(i * 256, 256), 256)
            left = pt[...].reshape(RH, NY * 2 * TOK)
            grad[q, :, columns] = jnp.dot(left, upv[:, columns], preferred_element_type=jnp.float32)
            return carry

        lax.fori_loop(0, FFL // 256, tile, 0)

    def block_of(q):
        def block(half, xo, zo):
            rows = pl.ds(pl.multiple_of((xo * NZ + zo) * BLK, BLK), BLK)
            start, width = (WA, WB // 2) if half else (0, WA // 2)
            parts = [grad[q, rows, pl.ds(start + i * width, width)] for i in range(2)]
            return jnp.concatenate(parts, axis=0)

        return block

    scatters = [
        Scatter(
            comm, ("rs", q), block_of(q),
            *(ref.at[q] for ref in (sa, ra, sb, rb, asum, sax, rax, sbz, rbz)),
        )
        for q in range(2)
    ]
    sums = [[None, None], [None, None]]

    def finish_half(q, half):
        value = scatters[q].last_b((0,)) if half else scatters[q].total_a()
        ys, yr = ((ysa, yra), (ysb, yrb))[half]
        ys[q] = value.astype(jnp.bfloat16)
        comm.send(("y", q, half), ys.at[q], yr.at[q], other_run)
        sums[q][half] = value

    def exchange(q):
        rows = pl.ds(q * BLK, BLK)
        for half, (yr, start, width) in enumerate(((yra, 0, WA // 2), (yrb, WA, WB // 2))):
            comm.recv(("y", q, half), yr.at[q], comm.dev())
            value = (sums[q][half] + yr[q].astype(jnp.float32)) * (1.0 / (NY * 2 * TOK * 64))
            for i in range(2):
                gsum[rows, pl.ds(start + i * width, width)] = value[i * BLK:(i + 1) * BLK]

    tasks = [(0.1, send_tokens), (16.4, recv_tokens), (22.3, up_copy.wait), (27.0, send_moments)]
    for q, late in ((0, 0.0), (1, 5.0)):
        tasks += [
            (0.0, functools.partial(send_mirror, q)),
            (late + 3.8, functools.partial(recv_mirror, q)),
        ]
        tasks += gather(
            comm, ("basis", q),
            lambda xo, zo, q=q: bfull.at[q, yh, xo, zo],
            lambda xo, zo, q=q: bfull.at[q, 1 - yh, xo, zo],
            late, late + 3.9,
        )
        tasks += [
            (late + 16.5, functools.partial(project, q)),
            (late + 21.0, functools.partial(collect, q)),
            (late + 22.4, functools.partial(product, q)),
        ]
        tasks += scatters[q].steps(late + 24.0)
        tasks += [
            (late + 35.5, functools.partial(finish_half, q, 1)),
            (late + 36.5, functools.partial(finish_half, q, 0)),
            (late + 41.5, functools.partial(exchange, q)),
        ]
    run(tasks)
    g = gsum[...]

    sq = jnp.sum(g * g, axis=0, keepdims=True)
    part = sq[:, 0:128]
    for i in range(1, FFL // 128):
        part = part + sq[:, i * 128:(i + 1) * 128]
    n1[0] = part
    for j in range(NX):
        for k in range(NZ):
            if j or k:
                comm.send(
                    ("n1", j, k), n1.at[0], n1.at[j * NZ + k],
                    comm.dev(x=wrap(x + j, NX), z=wrap(z + k, NZ)),
                )
    for j in range(NX):
        for k in range(NZ):
            if j or k:
                comm.recv(("n1", j, k), n1.at[j * NZ + k], comm.dev())
    n2[0] = jnp.sum(n1[...], axis=0)
    for r in range(NY):
        for e in range(2):
            if r or e:
                comm.send(
                    ("n2", r, e), n2.at[0], n2.at[r * 2 + e],
                    comm.dev(yl=wrap(yl + r, NY), c=lax.rem(c + e, 2)),
                )
    bas_copy.wait()
    row = lax.broadcasted_iota(jnp.int32, (R, R), 0)
    column = lax.broadcasted_iota(jnp.int32, (R, R), 1)
    source = ((column >> 3) & 1) * RH + (column >> 4) * BLK + (column & 7)
    pick = jnp.where(row == source, 1.0, 0.0).astype(jnp.bfloat16)
    bp[...] = jnp.dot(bas[...], pick, preferred_element_type=jnp.float32).astype(jnp.bfloat16)
    m_copy.wait()
    v_copy.wait()
    other_row0 = pl.multiple_of((1 - yh) * BLK, BLK)
    comm.recv("m", mom.at[0, pl.ds(other_row0, BLK)], comm.dev())
    comm.recv("v", mom.at[1, pl.ds(other_row0, BLK)], comm.dev())
    for r in range(NY):
        for e in range(2):
            if r or e:
                comm.recv(("n2", r, e), n2.at[r * 2 + e], comm.dev())
    norm = jnp.sqrt(jnp.sum(jnp.sum(n2[...], axis=0), axis=1, keepdims=True))
    clipped = g * jnp.minimum(1.0, 1.0 / norm)
    new_first = 0.9 * mom[0] + 0.1 * clipped
    new_second = 0.999 * mom[1] + 0.001 * clipped * clipped
    first_fix = 1.0 - 0.9**20
    second_fix = 1.0 - 0.999**20
    direction = (new_first / first_fix / (jnp.sqrt(new_second / second_fix) + 1e-08)).astype(jnp.bfloat16)
    da[x, z] = direction[:, :WA]
    db[x, z] = direction[:, WA:]

    run(gather(comm, "direction", lambda xo, zo: da.at[xo, zo], lambda xo, zo: db.at[xo, zo], 0.0, 0.0))
    for start, full, width in ((0, da, WA), (WA, db, WB)):
        out_ref[:, pl.ds(start, width)] = jnp.dot(
            bp[...], full[...].reshape(R, width), preferred_element_type=jnp.float32
        )
    comm.finish()


NSEM = 400


def local(tokens, up_cotangent, basis, first_moment, second_moment):
    bf, f32 = jnp.bfloat16, jnp.float32
    hbm_spec = pl.BlockSpec(memory_space=pltpu.HBM)
    vmem_spec = pl.BlockSpec(memory_space=pltpu.VMEM)
    return pl.pallas_call(
        kernel,
        out_shape=jax.ShapeDtypeStruct((BROWS, FFL), f32),
        in_specs=[hbm_spec] * 5,
        out_specs=vmem_spec,
        scratch_shapes=[
            pltpu.VMEM((2, TOK, 4096), bf),
            pltpu.VMEM((NY * 2 * TOK, FFL), bf),
            pltpu.VMEM((BROWS, R), bf),
            pltpu.VMEM((2, 2, NX, NZ, BROWS, RQ), bf),
            pltpu.VMEM((2, 2, NY, 2 * TOK, RQ), bf),
            pltpu.VMEM((2, RQ, NY * 2 * TOK), bf),
            pltpu.VMEM((2, RH, FFL), f32),
            pltpu.VMEM((2, 2 * BLK, FFL), f32),
            pltpu.VMEM((BROWS, R), bf),
            pltpu.VMEM((2, 2, 4, NX, 16, WA // 2), bf),
            pltpu.VMEM((2, 2, 4, NX, 16, WA // 2), bf),
            pltpu.VMEM((2, 2, 2, NZ, 16, WB // 2), bf),
            pltpu.VMEM((2, 2, 2, NZ, 16, WB // 2), bf),
            pltpu.VMEM((2, NX, 16, WA // 2), f32),
            pltpu.VMEM((2, NX, 16, WA // 2), bf),
            pltpu.VMEM((2, NX, 16, WA // 2), bf),
            pltpu.VMEM((2, NZ, 16, WB // 2), bf),
            pltpu.VMEM((2, NZ, 16, WB // 2), bf),
            pltpu.VMEM((2, 16, WA // 2), bf),
            pltpu.VMEM((2, 16, WA // 2), bf),
            pltpu.VMEM((2, 16, WB // 2), bf),
            pltpu.VMEM((2, 16, WB // 2), bf),
            pltpu.VMEM((2 * BLK, FFL), f32),
            pltpu.VMEM((NX * NZ, 1, 128), f32),
            pltpu.VMEM((NY * 2, 1, 128), f32),
            pltpu.VMEM((NX, NZ, 16, WA), bf),
            pltpu.VMEM((NX, NZ, 16, WB), bf),
            pltpu.SemaphoreType.DMA((7,)),
            pltpu.SemaphoreType.DMA((NSEM,)),
            pltpu.SemaphoreType.DMA((NSEM,)),
        ],
        compiler_params=pltpu.CompilerParams(
            collective_id=0, has_side_effects=True, vmem_limit_bytes=63 * 2**20
        ),
        cost_estimate=pl.CostEstimate(flops=4 * 10**9, bytes_accessed=2 * 10**7, transcendentals=0),
        name="galore_step",
    )(tokens, up_cotangent, basis, first_moment, second_moment)


def solution(mesh):
    in_specs = (
        P(("dp", "tensor"), None),
        P("dp", "tensor"),
        P("dp", None),
        P("dp", "tensor"),
        P("dp", "tensor"),
    )
    out_specs = P("dp", "tensor")
    return jax.shard_map(local, mesh=mesh, in_specs=in_specs, out_specs=out_specs, check_vma=False)
```

time: 115 us -> 114 us (level)
  the two profiles are of different devices: /device:TPU:4 before, /device:TPU:2 now
where the time goes in v3:
time: 114 us
  Pallas kernels  112 us (98%)
  local copies, waits for them, and re-layouts  1.82 us (2%)
    pallas_call x1, Pallas kernels, local(): pl.pallas_call(kernel, out_shape=jax.ShapeDtypeStruct((BROWS, FFL), f32),...  112 us

profile of v3, /device:TPU:2, one launch (start us, length us, event | category | flops | bytes accessed | tf_op | source)
XLA Modules:
  0.0 114.2 jit_solution(5696960431601727920)
XLA Ops:
  0.0 112.4 %galore_step.1 = f32[64,1792]{1,0:T(8,128)} custom-call(bf16[96,4096]{1,0:T(8,128)(2,1)} %tok_ref.1, bf16[768,1792]{1,0:T(8,128)(2,1)} %up_ref.1, bf16[64,512]{1,0:T(8,128)(2,1)} %basis_ref.1, f32[8,1792]{1,0:T(8,128)} %m_ref.1, f32[8,1792]{1,0:T(8,128)} %v_ref.1), custom_call_target="tpu_custom_call" | custom-call | flops 4000000000 | bytes 20000000 | tf_op jit(solution)/shard_map/galore_step/pallas_call | solution.py:466
  112.4 1.8 %copy.7 = f32[64,1792]{1,0:T(8,128)} copy(f32[64,1792]{1,0:T(8,128)} %galore_step.1) | data formatting | bytes 917504

commit v4 on v3

v4 whole, which is shorter than its diff:
```python
import functools

import jax
import jax.numpy as jnp
from jax import lax
from jax.experimental import pallas as pl
from jax.experimental.pallas import tpu as pltpu
from jax.sharding import PartitionSpec as P

MESH = pl.DeviceIdType.MESH
NX, NZ, NY = 4, 8, 4
BLK = 8
TOK = 96
FFL = 1792
WA, WB = 768, 1024
R = 512
RH = R // 2
RQ = RH // 2
BROWS = 64
X_ORDER = (0, 1, 3, 2)
Z_ORDER = (0, 1, -1, 2, -2, 3, -3, 4)
ZH = {1: (0, 1, 2, 3), -1: (-1, -2, -3, 4)}
XH = {1: (0, 1), -1: (3, 2)}
RZH = {1: (3, 1, 2, 0), -1: (4, -3, -1, -2)}
RXH = {1: (0, 2), -1: (1, 3)}
SIDES = (1, -1)


UNIT = 16 * 128 * 2
UNITS = 320


class Comm:
    def __init__(self, ssem, rsem, tally, coords):
        self.ssem, self.rsem, self.tally, self.coords = ssem, rsem, tally, coords
        self.groups, self.phases, self.coming, self.going = {}, {}, {}, {}

    def dev(self, yh=None, x=None, z=None, yl=None, c=None):
        own = self.coords
        yh, x, z, yl, c = (o if v is None else v for v, o in zip((yh, x, z, yl, c), own))
        return (yh * 32 + x * 8 + z, yl * 2 + c)

    def send(self, phase, group, src, dst, dev):
        i = self.phases.setdefault(phase, len(self.phases))
        j = self.groups.setdefault((phase, group), len(self.groups))
        pltpu.make_async_remote_copy(
            src_ref=src, dst_ref=dst, send_sem=self.ssem.at[i], recv_sem=self.rsem.at[j],
            device_id=dev, device_id_type=MESH,
        ).start()
        size = src.dtype.itemsize
        for n in src.shape:
            size *= n
        self.going[phase] = self.going.get(phase, 0) + size
        self.coming[phase, group] = self.coming.get((phase, group), 0) + size

    def total(self, size, ref):
        if ref is None:
            assert size % UNIT == 0 and size <= UNIT * UNITS
            ref = self.tally.at[pl.ds(0, size // UNIT)]
        return ref

    def wait(self, phase, group, ref=None):
        ref = self.total(self.coming.pop((phase, group)), ref)
        j = self.groups[phase, group]
        pltpu.make_async_remote_copy(
            src_ref=ref, dst_ref=ref, send_sem=self.ssem.at[0], recv_sem=self.rsem.at[j],
            device_id=self.dev(), device_id_type=MESH,
        ).wait_recv()

    def sent(self, phase, ref=None):
        ref = self.total(self.going.pop(phase), ref)
        pltpu.make_async_remote_copy(
            src_ref=ref, dst_ref=ref, send_sem=self.ssem.at[self.phases[phase]], recv_sem=self.rsem.at[0],
            device_id=self.dev(), device_id_type=MESH,
        ).wait_send()

    def finish(self):
        for phase in list(self.going):
            self.sent(phase)


def wrap(v, n):
    return lax.rem(v + n, n)


def run(tasks):
    for _, step in sorted(tasks, key=lambda task: task[0]):
        step()


def gather(comm, name, view_a, view_b, begin, begin_b):
    _, x, z, _, c = comm.coords
    turn = 1 - 2 * c

    def zs(k):
        return wrap(z + turn * k, NZ)

    near = {0: 0, 1: 1, 3: 1, 2: 2}
    far = {0: 0, 1: 1, -1: 1, 2: 2, -2: 2, 3: 3, -3: 3, 4: 3}
    name_a, name_b = (name, "a"), (name, "b")

    def send_ax():
        for j in X_ORDER[1:]:
            comm.send(name_a, ("x", near[j]), view_a(x, z), view_a(x, z), comm.dev(x=wrap(x + j, NX)))

    def ring_a(s, js):
        if s == 1 and js[0]:
            comm.wait(name_a, ("x", near[js[0]]))
        if 1 < s < 5:
            comm.wait(name_a, ("z", s - 1, near[js[0]]))
        if s == 5:
            comm.wait(name_a, ("z", 4))
            return
        for j in js:
            xo = wrap(x - j, NX)
            for side in SIDES:
                zo = wrap(z - side * (s - 1), NZ)
                if s < 4 or j in XH[side]:
                    group = ("z", s, near[j]) if s < 4 else ("z", 4)
                    comm.send(name_a, group, view_a(xo, zo), view_a(xo, zo), comm.dev(z=wrap(z + side, NZ)))

    def send_b(k, origin, hop):
        comm.send(name_b, ("z", far[k]), view_b(x, origin), view_b(x, origin), comm.dev(z=zs(hop)))

    def send_bz():
        for k in (2, -2, 1, -1):
            send_b(k, z, k)

    def ring_b1(ks):
        if ks[0]:
            comm.wait(name_b, ("z", far[ks[0]]))
        for k in ks:
            zo = zs(-k)
            if k == 2:
                send_b(3, zo, 1)
                send_b(4, zo, 2)
            if k == -2:
                send_b(-3, zo, -1)
            for side in SIDES:
                comm.send(name_b, ("x", far[k]), view_b(x, zo), view_b(x, zo), comm.dev(x=wrap(x + side, NX)))

    def ring_b2(ks):
        comm.wait(name_b, ("x", far[ks[0]]))
        for k in ks:
            zo = zs(-k)
            for side in SIDES:
                xo = wrap(x - side, NX)
                if k in ZH[side]:
                    comm.send(name_b, "x2", view_b(xo, zo), view_b(xo, zo), comm.dev(x=wrap(x + side, NX)))

    def last_b():
        comm.wait(name_b, "x2")

    steps_a = [
        (0.0, send_ax), (0.0, lambda: ring_a(1, (0,))),
        (2.3, lambda: ring_a(2, (0,))), (2.4, lambda: ring_a(1, (1, 3))), (2.9, lambda: ring_a(1, (2,))),
        (4.6, lambda: ring_a(3, (0,))), (4.7, lambda: ring_a(2, (1, 3))), (5.2, lambda: ring_a(2, (2,))),
        (7.0, lambda: ring_a(4, (0,))), (7.2, lambda: ring_a(3, (1, 3))), (7.6, lambda: ring_a(3, (2,))),
        (9.5, lambda: ring_a(4, (1, 3))), (9.9, lambda: ring_a(4, (2,))), (12.3, lambda: ring_a(5, X_ORDER)),
    ]
    steps_b = [
        (0.0, send_bz), (0.0, lambda: ring_b1((0,))),
        (2.3, lambda: ring_b1((1, -1))), (2.4, lambda: ring_b2((0,))), (3.0, lambda: ring_b1((2, -2))),
        (4.7, lambda: ring_b2((1, -1))), (5.4, lambda: ring_b2((2, -2))), (6.0, lambda: ring_b1((3, -3, 4))),
        (8.5, lambda: ring_b2((3, -3, 4))), (10.7, last_b),
    ]
    return [(begin + t, f) for t, f in steps_a] + [(begin_b + t, f) for t, f in steps_b]


class Scatter:
    def __init__(self, comm, name, block, sa, ra, sb, rb, asum, sax, rax, sbz, rbz):
        self.comm, self.name_a, self.name_b, self.block = comm, (name, "a"), (name, "b"), block
        self.last = {0: 0, 1: 1, -1: 1, 2: 2, -2: 2, 3: 3, -3: 3, 4: 3}
        self.sa, self.ra, self.sb, self.rb = sa, ra, sb, rb
        self.asum, self.sax, self.rax, self.sbz, self.rbz = asum, sax, rax, sbz, rbz
        _, self.x, self.z, _, c = comm.coords
        self.turn = 1 - 2 * c

    def zs(self, k):
        return wrap(self.z + self.turn * k, NZ)

    def step_a(self, s, prior):
        comm = self.comm
        if s >= 2 or prior and s:
            comm.wait(self.name_a, (s - 1, prior))
        for n, side in enumerate(SIDES):
            for j in RXH[side if prior else -side]:
                value = self.block(0, j, wrap(self.z + side * (4 - s), NZ))
                if s >= 2 or prior and s:
                    value = value + self.ra[n, s - 1, j].astype(jnp.float32)
                out = self.sa.at[n, s, j]
                out[...] = value.astype(jnp.bfloat16)
                group = (s, prior) if s < 3 else 3
                comm.send(self.name_a, group, out, self.ra.at[n, s, j], comm.dev(z=wrap(self.z + side, NZ)))

    def step_b(self, s, prior, part):
        comm = self.comm
        if s and prior:
            comm.wait(self.name_b, (0, part))
        for n, side in enumerate(SIDES):
            for k in RZH[side if prior else -side][2 * part:2 * part + 2]:
                value = self.block(1, wrap(self.x + side * (2 - s), NX), self.zs(k))
                if s and prior:
                    value = value + self.rb[n, 0, k % NZ].astype(jnp.float32)
                out = self.sb.at[n, s, k % NZ]
                out[...] = value.astype(jnp.bfloat16)
                group = (1, self.last[k]) if s else (0, part)
                comm.send(self.name_b, group, out, self.rb.at[n, s, k % NZ], comm.dev(x=wrap(self.x + side, NX)))

    def last_a(self):
        comm = self.comm
        comm.wait(self.name_a, 3)
        for j in range(NX):
            value = self.block(0, j, self.z)
            for n in range(2):
                value = value + self.ra[n, 3, j].astype(jnp.float32)
            self.asum[j] = value
            self.sax[j] = value.astype(jnp.bfloat16)
        for j in (2, 1, 3):
            xo = wrap(self.x + j, NX)
            comm.send(self.name_a, "x", self.sax.at[xo], self.rax.at[j], comm.dev(x=xo))

    def total_a(self):
        value = self.asum[self.x]
        self.comm.wait(self.name_a, "x")
        for j in (1, 3, 2):
            value = value + self.rax[j].astype(jnp.float32)
        return value

    def last_b(self, ks):
        comm = self.comm
        hop = {3: 1, -3: -1, 4: 2}
        plus = {2: (3, 4), -2: (-3,), 0: (1, -1, 2, -2)}
        comm.wait(self.name_b, (1, self.last[ks[0]]))
        if ks[0] in (0, 2):
            comm.wait(self.name_b, ("z", ks[0]))
        for k in ks:
            value = self.block(1, self.x, self.zs(k))
            for n in range(2):
                value = value + self.rb[n, 1, k % NZ].astype(jnp.float32)
            for other in plus.get(k, ()):
                value = value + self.rbz[other % NZ].astype(jnp.float32)
            if k == 0:
                return value
            self.sbz[k % NZ] = value.astype(jnp.bfloat16)
            comm.send(
                self.name_b, ("z", 2 if k in hop else 0), self.sbz.at[k % NZ], self.rbz.at[k % NZ],
                comm.dev(z=self.zs(hop.get(k, k))),
            )

    def steps(self, begin):
        a, b = self.step_a, self.step_b
        steps = [
            (0.0, lambda: a(0, True)), (0.0, lambda: b(0, True, 0)), (0.1, lambda: b(0, True, 1)),
            (0.2, lambda: a(1, False)), (0.3, lambda: b(1, False, 0)), (0.3, lambda: b(1, False, 1)),
            (2.3, lambda: a(1, True)), (2.5, lambda: a(2, False)),
            (2.6, lambda: b(1, True, 0)), (2.9, lambda: b(1, True, 1)),
            (4.6, lambda: a(2, True)), (4.9, lambda: a(3, False)),
            (5.2, lambda: self.last_b((4, 3, -3))), (5.8, lambda: self.last_b((1, -1))),
            (7.0, lambda: a(3, True)), (8.5, lambda: self.last_b((2, -2))), (9.4, self.last_a),
        ]
        return [(begin + t, f) for t, f in steps]


def kernel(
    tok_ref, up_ref, basis_ref, m_ref, v_ref, out_ref,
    toks, upv, bas, bfull, pall, pt, grad, mom, bp,
    sa, ra, sb, rb, asum, sax, rax, sbz, rbz, ysa, yra, ysb, yrb, gsum, n1, n2, da, db,
    tally, lsem, ssem, rsem,
):
    d, t = lax.axis_index("dp"), lax.axis_index("tensor")
    yh, x, z, yl, c = lax.div(d, 32), lax.rem(lax.div(d, 8), 4), lax.rem(d, 8), lax.div(t, 2), lax.rem(t, 2)
    comm = Comm(ssem, rsem, tally, (yh, x, z, yl, c))
    other_core = comm.dev(c=1 - c)
    other_run = comm.dev(yh=1 - yh)
    mirror = comm.dev(yh=1 - yh, yl=3 - yl)

    b_copies = []
    for q in range(2):
        columns = pl.ds(pl.multiple_of(q * RH + c * RQ, RQ), RQ)
        b_copies.append(pltpu.make_async_copy(basis_ref.at[:, columns], bfull.at[q, yh, x, z], lsem.at[5 + q]))
        b_copies[q].start()
    barrier = pltpu.get_barrier_semaphore()
    peers = [other_core, mirror]
    peers += [comm.dev(x=wrap(x + j, NX)) for j in range(1, NX)]
    peers += [comm.dev(z=wrap(z + k, NZ)) for k in (1, -1, 2, -2)]
    peers += [comm.dev(yl=wrap(yl + r, NY)) for r in range(1, NY)]
    for peer in peers:
        pl.semaphore_signal(barrier, inc=1, device_id=peer, device_id_type=MESH)

    row0 = pl.multiple_of(yh * BLK, BLK)
    tok_copy = pltpu.make_async_copy(tok_ref, toks.at[c], lsem.at[0])
    up_copy = pltpu.make_async_copy(up_ref, upv, lsem.at[1])
    m_copy = pltpu.make_async_copy(m_ref, mom.at[0, pl.ds(row0, BLK)], lsem.at[2])
    v_copy = pltpu.make_async_copy(v_ref, mom.at[1, pl.ds(row0, BLK)], lsem.at[3])
    bas_copy = pltpu.make_async_copy(basis_ref, bas, lsem.at[4])
    for copy in b_copies:
        copy.wait()
    pl.semaphore_wait(barrier, len(peers))

    def send_mirror(q):
        comm.send("mirror", q, bfull.at[q, yh, x, z], bfull.at[q, yh, x, z], mirror)

    def recv_mirror(q):
        comm.wait("mirror", q)

    def load_rest():
        for copy in (up_copy, m_copy, v_copy, bas_copy):
            copy.start()

    def send_tokens():
        tok_copy.start()
        comm.send("tok", 0, tok_ref, toks.at[c], other_core)

    def recv_tokens():
        tok_copy.wait()
        comm.wait("tok", 0)

    def send_moments():
        comm.send("moments", 0, m_ref, mom.at[0, pl.ds(row0, BLK)], other_run)
        comm.send("moments", 0, v_ref, mom.at[1, pl.ds(row0, BLK)], other_run)

    def project(q):
        proj = jnp.zeros((2 * TOK, RQ), jnp.float32)
        depth = NZ * BROWS
        for a in range(2):
            for b in range(NX):
                left = toks[:, :, pl.ds((a * NX + b) * depth, depth)].reshape(2 * TOK, depth)
                proj += jnp.dot(left, bfull[q, a, b].reshape(depth, RQ), preferred_element_type=jnp.float32)
        piece = pall.at[q, c, yl]
        piece[...] = proj.astype(jnp.bfloat16)
        for r in (2, 1, 3):
            comm.send("p", (q, r % 2), piece, piece, comm.dev(yl=wrap(yl + r, NY)))
        comm.send("core", q, piece, piece, other_core)

    def collect(q):
        for r in (1, 3, 2):
            piece = pall.at[q, c, wrap(yl - r, NY)]
            if r != 3:
                comm.wait("p", (q, r % 2))
            comm.send("core", q, piece, piece, other_core)

    def product(q):
        comm.wait("core", q)
        for half in range(2):
            pt[half] = pall[q, half].reshape(NY * 2 * TOK, RQ).T

        def tile(i, carry):
            columns = pl.ds(pl.multiple_of(i * 256, 256), 256)
            left = pt[...].reshape(RH, NY * 2 * TOK)
            grad[q, :, columns] = jnp.dot(left, upv[:, columns], preferred_element_type=jnp.float32)
            return carry

        lax.fori_loop(0, FFL // 256, tile, 0)

    def block_of(q):
        def block(half, xo, zo):
            rows = pl.ds(pl.multiple_of((xo * NZ + zo) * BLK, BLK), BLK)
            start, width = (WA, WB // 2) if half else (0, WA // 2)
            parts = [grad[q, rows, pl.ds(start + i * width, width)] for i in range(2)]
            return jnp.concatenate(parts, axis=0)

        return block

    scatters = [
        Scatter(
            comm, ("rs", q), block_of(q),
            *(ref.at[q] for ref in (sa, ra, sb, rb, asum, sax, rax, sbz, rbz)),
        )
        for q in range(2)
    ]
    sums = [[None, None], [None, None]]

    def finish_half(q, half):
        value = scatters[q].last_b((0,)) if half else scatters[q].total_a()
        ys, yr = ((ysa, yra), (ysb, yrb))[half]
        ys[q] = value.astype(jnp.bfloat16)
        comm.send("y", (q, half), ys.at[q], yr.at[q], other_run)
        sums[q][half] = value

    def exchange(q):
        rows = pl.ds(q * BLK, BLK)
        for half, (yr, start, width) in enumerate(((yra, 0, WA // 2), (yrb, WA, WB // 2))):
            comm.wait("y", (q, half))
            value = (sums[q][half] + yr[q].astype(jnp.float32)) * (1.0 / (NY * 2 * TOK * 64))
            for i in range(2):
                gsum[rows, pl.ds(start + i * width, width)] = value[i * BLK:(i + 1) * BLK]

    tasks = [(2.0, send_tokens), (7.0, load_rest), (16.4, recv_tokens), (22.3, up_copy.wait), (27.0, send_moments)]
    for q, late in ((0, 0.0), (1, 5.0)):
        tasks += [
            (0.0, functools.partial(send_mirror, q)),
            (late + 3.8, functools.partial(recv_mirror, q)),
        ]
        tasks += gather(
            comm, ("basis", q),
            lambda xo, zo, q=q: bfull.at[q, yh, xo, zo],
            lambda xo, zo, q=q: bfull.at[q, 1 - yh, xo, zo],
            late, late + 3.9,
        )
        tasks += [
            (late + 16.5, functools.partial(project, q)),
            (late + 21.0, functools.partial(collect, q)),
            (late + 22.4, functools.partial(product, q)),
        ]
        tasks += scatters[q].steps(late + 24.0)
        tasks += [
            (late + 35.5, functools.partial(finish_half, q, 1)),
            (late + 36.5, functools.partial(finish_half, q, 0)),
            (late + 41.5, functools.partial(exchange, q)),
        ]
    run(tasks)
    g = gsum[...]

    sq = jnp.sum(g * g, axis=0, keepdims=True)
    part = sq[:, 0:128]
    for i in range(1, FFL // 128):
        part = part + sq[:, i * 128:(i + 1) * 128]
    n1[0] = part
    for j in range(NX):
        for k in range(NZ):
            if j or k:
                comm.send(
                    "n1", 0, n1.at[0], n1.at[j * NZ + k],
                    comm.dev(x=wrap(x + j, NX), z=wrap(z + k, NZ)),
                )
    comm.wait("n1", 0, n1.at[pl.ds(1, NX * NZ - 1)])
    n2[0] = jnp.sum(n1[...], axis=0)
    for r in range(NY):
        for e in range(2):
            if r or e:
                comm.send(
                    "n2", 0, n2.at[0], n2.at[r * 2 + e],
                    comm.dev(yl=wrap(yl + r, NY), c=lax.rem(c + e, 2)),
                )
    bas_copy.wait()
    row = lax.broadcasted_iota(jnp.int32, (R, R), 0)
    column = lax.broadcasted_iota(jnp.int32, (R, R), 1)
    source = ((column >> 3) & 1) * RH + (column >> 4) * BLK + (column & 7)
    pick = jnp.where(row == source, 1.0, 0.0).astype(jnp.bfloat16)
    bp[...] = jnp.dot(bas[...], pick, preferred_element_type=jnp.float32).astype(jnp.bfloat16)
    m_copy.wait()
    v_copy.wait()
    comm.wait("moments", 0)
    comm.wait("n2", 0, n2.at[pl.ds(1, NY * 2 - 1)])
    norm = jnp.sqrt(jnp.sum(jnp.sum(n2[...], axis=0), axis=1, keepdims=True))
    clipped = g * jnp.minimum(1.0, 1.0 / norm)
    new_first = 0.9 * mom[0] + 0.1 * clipped
    new_second = 0.999 * mom[1] + 0.001 * clipped * clipped
    first_fix = 1.0 - 0.9**20
    second_fix = 1.0 - 0.999**20
    direction = (new_first / first_fix / (jnp.sqrt(new_second / second_fix) + 1e-08)).astype(jnp.bfloat16)
    da[x, z] = direction[:, :WA]
    db[x, z] = direction[:, WA:]

    run(gather(comm, "direction", lambda xo, zo: da.at[xo, zo], lambda xo, zo: db.at[xo, zo], 0.0, 0.0))
    for start, full, width in ((0, da, WA), (WA, db, WB)):
        out_ref[:, pl.ds(start, width)] = jnp.dot(
            bp[...], full[...].reshape(R, width), preferred_element_type=jnp.float32
        )
    comm.sent("n1", n1.at[pl.ds(1, NX * NZ - 1)])
    comm.sent("n2", n2.at[pl.ds(1, NY * 2 - 1)])
    comm.finish()


N_PHASES, N_GROUPS = 18, 108


def local(tokens, up_cotangent, basis, first_moment, second_moment):
    bf, f32 = jnp.bfloat16, jnp.float32
    hbm_spec = pl.BlockSpec(memory_space=pltpu.HBM)
    vmem_spec = pl.BlockSpec(memory_space=pltpu.VMEM)
    return pl.pallas_call(
        kernel,
        out_shape=jax.ShapeDtypeStruct((BROWS, FFL), f32),
        in_specs=[hbm_spec] * 5,
        out_specs=vmem_spec,
        scratch_shapes=[
            pltpu.VMEM((2, TOK, 4096), bf),
            pltpu.VMEM((NY * 2 * TOK, FFL), bf),
            pltpu.VMEM((BROWS, R), bf),
            pltpu.VMEM((2, 2, NX, NZ, BROWS, RQ), bf),
            pltpu.VMEM((2, 2, NY, 2 * TOK, RQ), bf),
            pltpu.VMEM((2, RQ, NY * 2 * TOK), bf),
            pltpu.VMEM((2, RH, FFL), f32),
            pltpu.VMEM((2, 2 * BLK, FFL), f32),
            pltpu.VMEM((BROWS, R), bf),
            pltpu.VMEM((2, 2, 4, NX, 16, WA // 2), bf),
            pltpu.VMEM((2, 2, 4, NX, 16, WA // 2), bf),
            pltpu.VMEM((2, 2, 2, NZ, 16, WB // 2), bf),
            pltpu.VMEM((2, 2, 2, NZ, 16, WB // 2), bf),
            pltpu.VMEM((2, NX, 16, WA // 2), f32),
            pltpu.VMEM((2, NX, 16, WA // 2), bf),
            pltpu.VMEM((2, NX, 16, WA // 2), bf),
            pltpu.VMEM((2, NZ, 16, WB // 2), bf),
            pltpu.VMEM((2, NZ, 16, WB // 2), bf),
            pltpu.VMEM((2, 16, WA // 2), bf),
            pltpu.VMEM((2, 16, WA // 2), bf),
            pltpu.VMEM((2, 16, WB // 2), bf),
            pltpu.VMEM((2, 16, WB // 2), bf),
            pltpu.VMEM((2 * BLK, FFL), f32),
            pltpu.VMEM((NX * NZ, 1, 128), f32),
            pltpu.VMEM((NY * 2, 1, 128), f32),
            pltpu.VMEM((NX, NZ, 16, WA), bf),
            pltpu.VMEM((NX, NZ, 16, WB), bf),
            pltpu.VMEM((UNITS, 16, 128), bf),
            pltpu.SemaphoreType.DMA((7,)),
            pltpu.SemaphoreType.DMA((N_PHASES,)),
            pltpu.SemaphoreType.DMA((N_GROUPS,)),
        ],
        compiler_params=pltpu.CompilerParams(
            collective_id=0, has_side_effects=True, vmem_limit_bytes=63 * 2**20
        ),
        cost_estimate=pl.CostEstimate(flops=4 * 10**9, bytes_accessed=2 * 10**7, transcendentals=0),
        name="galore_step",
    )(tokens, up_cotangent, basis, first_moment, second_moment)


def solution(mesh):
    in_specs = (
        P(("dp", "tensor"), None),
        P("dp", "tensor"),
        P("dp", None),
        P("dp", "tensor"),
        P("dp", "tensor"),
    )
    out_specs = P("dp", "tensor")
    return jax.shard_map(local, mesh=mesh, in_specs=in_specs, out_specs=out_specs, check_vma=False)
```

time: 114 us -> 110 us (0.965)
  Pallas kernels: 112 us -> 108 us
    pallas_call x1, Pallas kernels: 112 us -> 108 us  [local(): pl.pallas_call(kernel, out_shape=jax.ShapeDtypeStruct((BROWS, FFL), f32),...]
where the time goes in v4:
time: 110 us
  Pallas kernels  108 us (98%)
  local copies, waits for them, and re-layouts  1.82 us (2%)
    pallas_call x1, Pallas kernels, local(): pl.pallas_call(kernel, out_shape=jax.ShapeDtypeStruct((BROWS, FFL), f32),...  108 us

profile of v4, /device:TPU:2, one launch (start us, length us, event | category | flops | bytes accessed | tf_op | source)
XLA Modules:
  0.0 109.9 jit_solution(5126511457926277883)
XLA Ops:
  0.0 108.1 %galore_step.1 = f32[64,1792]{1,0:T(8,128)} custom-call(bf16[96,4096]{1,0:T(8,128)(2,1)} %tok_ref.1, bf16[768,1792]{1,0:T(8,128)(2,1)} %up_ref.1, bf16[64,512]{1,0:T(8,128)(2,1)} %basis_ref.1, f32[8,1792]{1,0:T(8,128)} %m_ref.1, f32[8,1792]{1,0:T(8,128)} %v_ref.1), custom_call_target="tpu_custom_call" | custom-call | flops 4000000000 | bytes 20000000 | tf_op jit(solution)/shard_map/galore_step/pallas_call | solution.py:473
  108.1 1.8 %copy.7 = f32[64,1792]{1,0:T(8,128)} copy(f32[64,1792]{1,0:T(8,128)} %galore_step.1) | data formatting | bytes 917504

commit v5 on v4

--- a/solution.py
+++ b/solution.py
@@ -164,7 +164,7 @@
         (4.7, lambda: ring_b2((1, -1))), (5.4, lambda: ring_b2((2, -2))), (6.0, lambda: ring_b1((3, -3, 4))),
         (8.5, lambda: ring_b2((3, -3, 4))), (10.7, last_b),
     ]
-    return [(begin + t, f) for t, f in steps_a] + [(begin_b + t, f) for t, f in steps_b]
+    return [(begin + 1.4 * t, f) for t, f in steps_a] + [(begin_b + 1.4 * t, f) for t, f in steps_b]
 
 
 class Scatter:
@@ -259,7 +259,7 @@
             (5.2, lambda: self.last_b((4, 3, -3))), (5.8, lambda: self.last_b((1, -1))),
             (7.0, lambda: a(3, True)), (8.5, lambda: self.last_b((2, -2))), (9.4, self.last_a),
         ]
-        return [(begin + t, f) for t, f in steps]
+        return [(begin + 1.3 * t, f) for t, f in steps]
 
 
 def kernel(
@@ -386,28 +386,28 @@
             for i in range(2):
                 gsum[rows, pl.ds(start + i * width, width)] = value[i * BLK:(i + 1) * BLK]
 
-    tasks = [(2.0, send_tokens), (7.0, load_rest), (16.4, recv_tokens), (22.3, up_copy.wait), (27.0, send_moments)]
-    for q, late in ((0, 0.0), (1, 5.0)):
+    tasks = [(2.0, send_tokens), (7.0, load_rest), (19.6, recv_tokens), (27.2, up_copy.wait), (37.0, send_moments)]
+    for q, late in ((0, 0.0), (1, 7.5)):
         tasks += [
-            (0.0, functools.partial(send_mirror, q)),
-            (late + 3.8, functools.partial(recv_mirror, q)),
+            (0.6 * late, functools.partial(send_mirror, q)),
+            (late + 4.4, functools.partial(recv_mirror, q)),
         ]
         tasks += gather(
             comm, ("basis", q),
             lambda xo, zo, q=q: bfull.at[q, yh, xo, zo],
             lambda xo, zo, q=q: bfull.at[q, 1 - yh, xo, zo],
-            late, late + 3.9,
+            late, late + 4.5,
         )
         tasks += [
-            (late + 16.5, functools.partial(project, q)),
-            (late + 21.0, functools.partial(collect, q)),
-            (late + 22.4, functools.partial(product, q)),
+            (late + 19.7, functools.partial(project, q)),
+            (late + 25.7, functools.partial(collect, q)),
+            (late + 27.3, functools.partial(product, q)),
         ]
-        tasks += scatters[q].steps(late + 24.0)
+        tasks += scatters[q].steps(late + 28.8)
         tasks += [
-            (late + 35.5, functools.partial(finish_half, q, 1)),
-            (late + 36.5, functools.partial(finish_half, q, 0)),
-            (late + 41.5, functools.partial(exchange, q)),
+            (late + 43.8, functools.partial(finish_half, q, 1)),
+            (late + 45.0, functools.partial(finish_half, q, 0)),
+            (late + 50.0, functools.partial(exchange, q)),
         ]
     run(tasks)
     g = gsum[...]

time: 110 us -> 110 us (level)
  the two profiles are of different devices: /device:TPU:2 before, /device:TPU:16 now
where the time goes in v5:
time: 110 us
  Pallas kernels  108 us (98%)
  local copies, waits for them, and re-layouts  1.82 us (2%)
    pallas_call x1, Pallas kernels, local(): pl.pallas_call(kernel, out_shape=jax.ShapeDtypeStruct((BROWS, FFL), f32),...  108 us

profile of v5, /device:TPU:16, one launch (start us, length us, event | category | flops | bytes accessed | tf_op | source)
XLA Modules:
  0.0 110.2 jit_solution(13433828342301111155)
XLA Ops:
  0.0 108.4 %galore_step.1 = f32[64,1792]{1,0:T(8,128)} custom-call(bf16[96,4096]{1,0:T(8,128)(2,1)} %tok_ref.1, bf16[768,1792]{1,0:T(8,128)(2,1)} %up_ref.1, bf16[64,512]{1,0:T(8,128)(2,1)} %basis_ref.1, f32[8,1792]{1,0:T(8,128)} %m_ref.1, f32[8,1792]{1,0:T(8,128)} %v_ref.1), custom_call_target="tpu_custom_call" | custom-call | flops 4000000000 | bytes 20000000 | tf_op jit(solution)/shard_map/galore_step/pallas_call | solution.py:473
  108.4 1.8 %copy.7 = f32[64,1792]{1,0:T(8,128)} copy(f32[64,1792]{1,0:T(8,128)} %galore_step.1) | data formatting | bytes 917504

commit v6 on v5

--- a/solution.py
+++ b/solution.py
@@ -12,17 +12,15 @@
 BLK = 8
 TOK = 96
 FFL = 1792
-WA, WB = 768, 1024
+WA, WB = 512, 1280
+DA, DB = 640, 1152
 R = 512
 RH = R // 2
 RQ = RH // 2
 BROWS = 64
 X_ORDER = (0, 1, 3, 2)
 Z_ORDER = (0, 1, -1, 2, -2, 3, -3, 4)
-ZH = {1: (0, 1, 2, 3), -1: (-1, -2, -3, 4)}
-XH = {1: (0, 1), -1: (3, 2)}
 RZH = {1: (3, 1, 2, 0), -1: (4, -3, -1, -2)}
-RXH = {1: (0, 2), -1: (1, 3)}
 SIDES = (1, -1)
 
 
@@ -103,21 +101,27 @@
         for j in X_ORDER[1:]:
             comm.send(name_a, ("x", near[j]), view_a(x, z), view_a(x, z), comm.dev(x=wrap(x + j, NX)))
 
-    def ring_a(s, js):
-        if s == 1 and js[0]:
+    def pass_a(xo, origin, hop, group):
+        comm.send(name_a, group, view_a(xo, origin), view_a(xo, origin), comm.dev(z=zs(hop)))
+
+    def near_a(js):
+        if js[0]:
             comm.wait(name_a, ("x", near[js[0]]))
-        if 1 < s < 5:
-            comm.wait(name_a, ("z", s - 1, near[js[0]]))
-        if s == 5:
-            comm.wait(name_a, ("z", 4))
-            return
         for j in js:
             xo = wrap(x - j, NX)
-            for side in SIDES:
-                zo = wrap(z - side * (s - 1), NZ)
-                if s < 4 or j in XH[side]:
-                    group = ("z", s, near[j]) if s < 4 else ("z", 4)
-                    comm.send(name_a, group, view_a(xo, zo), view_a(xo, zo), comm.dev(z=wrap(z + side, NZ)))
+            for hop in (2, -2, 1, -1):
+                pass_a(xo, z, hop, ("z", near[j]) if hop in (2, -2) else "z")
+
+    def far_a(js):
+        comm.wait(name_a, ("z", near[js[0]]))
+        for j in js:
+            xo = wrap(x - j, NX)
+            pass_a(xo, zs(-2), 2, "z")
+            pass_a(xo, zs(-2), 1, "z")
+            pass_a(xo, zs(2), -1, "z")
+
+    def last_a():
+        comm.wait(name_a, "z")
 
     def send_b(k, origin, hop):
         comm.send(name_b, ("z", far[k]), view_b(x, origin), view_b(x, origin), comm.dev(z=zs(hop)))
@@ -126,45 +130,33 @@
         for k in (2, -2, 1, -1):
             send_b(k, z, k)
 
-    def ring_b1(ks):
+    def cross_b(ks):
         if ks[0]:
             comm.wait(name_b, ("z", far[ks[0]]))
         for k in ks:
             zo = zs(-k)
             if k == 2:
+                send_b(4, zo, 2)
                 send_b(3, zo, 1)
-                send_b(4, zo, 2)
             if k == -2:
                 send_b(-3, zo, -1)
-            for side in SIDES:
-                comm.send(name_b, ("x", far[k]), view_b(x, zo), view_b(x, zo), comm.dev(x=wrap(x + side, NX)))
-
-    def ring_b2(ks):
-        comm.wait(name_b, ("x", far[ks[0]]))
         for k in ks:
             zo = zs(-k)
-            for side in SIDES:
-                xo = wrap(x - side, NX)
-                if k in ZH[side]:
-                    comm.send(name_b, "x2", view_b(xo, zo), view_b(xo, zo), comm.dev(x=wrap(x + side, NX)))
+            for j in X_ORDER[1:]:
+                comm.send(name_b, "x", view_b(x, zo), view_b(x, zo), comm.dev(x=wrap(x + j, NX)))
 
     def last_b():
-        comm.wait(name_b, "x2")
+        comm.wait(name_b, "x")
 
     steps_a = [
-        (0.0, send_ax), (0.0, lambda: ring_a(1, (0,))),
-        (2.3, lambda: ring_a(2, (0,))), (2.4, lambda: ring_a(1, (1, 3))), (2.9, lambda: ring_a(1, (2,))),
-        (4.6, lambda: ring_a(3, (0,))), (4.7, lambda: ring_a(2, (1, 3))), (5.2, lambda: ring_a(2, (2,))),
-        (7.0, lambda: ring_a(4, (0,))), (7.2, lambda: ring_a(3, (1, 3))), (7.6, lambda: ring_a(3, (2,))),
-        (9.5, lambda: ring_a(4, (1, 3))), (9.9, lambda: ring_a(4, (2,))), (12.3, lambda: ring_a(5, X_ORDER)),
+        (0.0, send_ax), (0.0, lambda: near_a((0,))), (2.8, lambda: near_a((1, 3))), (3.3, lambda: far_a((0,))),
+        (3.4, lambda: near_a((2,))), (6.2, lambda: far_a((1, 3))), (6.9, lambda: far_a((2,))), (11.0, last_a),
     ]
     steps_b = [
-        (0.0, send_bz), (0.0, lambda: ring_b1((0,))),
-        (2.3, lambda: ring_b1((1, -1))), (2.4, lambda: ring_b2((0,))), (3.0, lambda: ring_b1((2, -2))),
-        (4.7, lambda: ring_b2((1, -1))), (5.4, lambda: ring_b2((2, -2))), (6.0, lambda: ring_b1((3, -3, 4))),
-        (8.5, lambda: ring_b2((3, -3, 4))), (10.7, last_b),
+        (0.0, send_bz), (0.0, lambda: cross_b((0,))), (3.3, lambda: cross_b((2, -2))), (3.4, lambda: cross_b((1, -1))),
+        (6.8, lambda: cross_b((4, 3, -3))), (11.0, last_b),
     ]
-    return [(begin + 1.4 * t, f) for t, f in steps_a] + [(begin_b + 1.4 * t, f) for t, f in steps_b]
+    return [(begin + t, f) for t, f in steps_a] + [(begin_b + t, f) for t, f in steps_b]
 
 
 class Scatter:
@@ -179,19 +171,30 @@
     def zs(self, k):
         return wrap(self.z + self.turn * k, NZ)
 
-    def step_a(self, s, prior):
-        comm = self.comm
-        if s >= 2 or prior and s:
-            comm.wait(self.name_a, (s - 1, prior))
-        for n, side in enumerate(SIDES):
-            for j in RXH[side if prior else -side]:
-                value = self.block(0, j, wrap(self.z + side * (4 - s), NZ))
-                if s >= 2 or prior and s:
-                    value = value + self.ra[n, s - 1, j].astype(jnp.float32)
-                out = self.sa.at[n, s, j]
-                out[...] = value.astype(jnp.bfloat16)
-                group = (s, prior) if s < 3 else 3
-                comm.send(self.name_a, group, out, self.ra.at[n, s, j], comm.dev(z=wrap(self.z + side, NZ)))
+    def pass_a(self, j, k, hop, others, group):
+        value = self.block(0, j, self.zs(k))
+        for other in others:
+            value = value + self.ra[other % NZ, j].astype(jnp.float32)
+        out = self.sa.at[k % NZ, j]
+        out[...] = value.astype(jnp.bfloat16)
+        self.comm.send(self.name_a, group, out, self.ra.at[k % NZ, j], self.comm.dev(z=self.zs(hop)))
+
+    def far_a(self, part):
+        for j in (2 * part, 2 * part + 1):
+            self.pass_a(j, 4, 2, (), ("far", part))
+            self.pass_a(j, 3, 1, (), ("far", part))
+            self.pass_a(j, -3, -1, (), ("far", part))
+
+    def near_a(self, part):
+        for j in (2 * part, 2 * part + 1):
+            self.pass_a(j, 1, 1, (), "near")
+            self.pass_a(j, -1, -1, (), "near")
+
+    def mid_a(self, part):
+        self.comm.wait(self.name_a, ("far", part))
+        for j in (2 * part, 2 * part + 1):
+            self.pass_a(j, 2, 2, (3, 4), "near")
+            self.pass_a(j, -2, -2, (-3,), "near")
 
     def step_b(self, s, prior, part):
         comm = self.comm
@@ -209,11 +212,11 @@
 
     def last_a(self):
         comm = self.comm
-        comm.wait(self.name_a, 3)
+        comm.wait(self.name_a, "near")
         for j in range(NX):
             value = self.block(0, j, self.z)
-            for n in range(2):
-                value = value + self.ra[n, 3, j].astype(jnp.float32)
+            for k in (1, -1, 2, -2):
+                value = value + self.ra[k % NZ, j].astype(jnp.float32)
             self.asum[j] = value
             self.sax[j] = value.astype(jnp.bfloat16)
         for j in (2, 1, 3):
@@ -249,17 +252,17 @@
             )
 
     def steps(self, begin):
-        a, b = self.step_a, self.step_b
+        b = self.step_b
         steps = [
-            (0.0, lambda: a(0, True)), (0.0, lambda: b(0, True, 0)), (0.1, lambda: b(0, True, 1)),
-            (0.2, lambda: a(1, False)), (0.3, lambda: b(1, False, 0)), (0.3, lambda: b(1, False, 1)),
-            (2.3, lambda: a(1, True)), (2.5, lambda: a(2, False)),
-            (2.6, lambda: b(1, True, 0)), (2.9, lambda: b(1, True, 1)),
-            (4.6, lambda: a(2, True)), (4.9, lambda: a(3, False)),
-            (5.2, lambda: self.last_b((4, 3, -3))), (5.8, lambda: self.last_b((1, -1))),
-            (7.0, lambda: a(3, True)), (8.5, lambda: self.last_b((2, -2))), (9.4, self.last_a),
+            (0.0, lambda: self.far_a(0)), (0.1, lambda: b(0, True, 0)), (0.2, lambda: self.far_a(1)),
+            (0.3, lambda: b(0, True, 1)), (0.4, lambda: self.near_a(0)), (0.5, lambda: b(1, False, 0)),
+            (0.6, lambda: self.near_a(1)), (0.7, lambda: b(1, False, 1)),
+            (3.4, lambda: self.mid_a(0)), (3.5, lambda: b(1, True, 0)),
+            (3.6, lambda: self.mid_a(1)), (3.8, lambda: b(1, True, 1)),
+            (6.9, self.last_a), (7.0, lambda: self.last_b((4, 3, -3))), (7.5, lambda: self.last_b((1, -1))),
+            (10.4, lambda: self.last_b((2, -2))),
         ]
-        return [(begin + 1.3 * t, f) for t, f in steps]
+        return [(begin + t, f) for t, f in steps]
 
 
 def kernel(
@@ -386,10 +389,10 @@
             for i in range(2):
                 gsum[rows, pl.ds(start + i * width, width)] = value[i * BLK:(i + 1) * BLK]
 
-    tasks = [(2.0, send_tokens), (7.0, load_rest), (19.6, recv_tokens), (27.2, up_copy.wait), (37.0, send_moments)]
-    for q, late in ((0, 0.0), (1, 7.5)):
+    tasks = [(2.0, send_tokens), (6.0, load_rest), (15.9, recv_tokens), (22.9, up_copy.wait), (32.0, send_moments)]
+    for q, late in ((0, 0.0), (1, 6.5)):
         tasks += [
-            (0.6 * late, functools.partial(send_mirror, q)),
+            (0.3 * late, functools.partial(send_mirror, q)),
             (late + 4.4, functools.partial(recv_mirror, q)),
         ]
         tasks += gather(
@@ -399,15 +402,15 @@
             late, late + 4.5,
         )
         tasks += [
-            (late + 19.7, functools.partial(project, q)),
-            (late + 25.7, functools.partial(collect, q)),
-            (late + 27.3, functools.partial(product, q)),
+            (late + 16.0, functools.partial(project, q)),
+            (late + 21.5, functools.partial(collect, q)),
+            (late + 23.0, functools.partial(product, q)),
         ]
-        tasks += scatters[q].steps(late + 28.8)
+        tasks += scatters[q].steps(late + 24.5)
         tasks += [
-            (late + 43.8, functools.partial(finish_half, q, 1)),
-            (late + 45.0, functools.partial(finish_half, q, 0)),
-            (late + 50.0, functools.partial(exchange, q)),
+            (late + 38.0, functools.partial(finish_half, q, 1)),
+            (late + 34.8, functools.partial(finish_half, q, 0)),
+            (late + 43.0, functools.partial(exchange, q)),
         ]
     run(tasks)
     g = gsum[...]
@@ -450,11 +453,11 @@
     first_fix = 1.0 - 0.9**20
     second_fix = 1.0 - 0.999**20
     direction = (new_first / first_fix / (jnp.sqrt(new_second / second_fix) + 1e-08)).astype(jnp.bfloat16)
-    da[x, z] = direction[:, :WA]
-    db[x, z] = direction[:, WA:]
+    da[x, z] = direction[:, :DA]
+    db[x, z] = direction[:, DA:]
 
     run(gather(comm, "direction", lambda xo, zo: da.at[xo, zo], lambda xo, zo: db.at[xo, zo], 0.0, 0.0))
-    for start, full, width in ((0, da, WA), (WA, db, WB)):
+    for start, full, width in ((0, da, DA), (DA, db, DB)):
         out_ref[:, pl.ds(start, width)] = jnp.dot(
             bp[...], full[...].reshape(R, width), preferred_element_type=jnp.float32
         )
@@ -463,7 +466,7 @@
     comm.finish()
 
 
-N_PHASES, N_GROUPS = 18, 108
+N_PHASES, N_GROUPS = 18, 70
 
 
 def local(tokens, up_cotangent, basis, first_moment, second_moment):
@@ -485,8 +488,8 @@
             pltpu.VMEM((2, RH, FFL), f32),
             pltpu.VMEM((2, 2 * BLK, FFL), f32),
             pltpu.VMEM((BROWS, R), bf),
-            pltpu.VMEM((2, 2, 4, NX, 16, WA // 2), bf),
-            pltpu.VMEM((2, 2, 4, NX, 16, WA // 2), bf),
+            pltpu.VMEM((2, NZ, NX, 16, WA // 2), bf),
+            pltpu.VMEM((2, NZ, NX, 16, WA // 2), bf),
             pltpu.VMEM((2, 2, 2, NZ, 16, WB // 2), bf),
             pltpu.VMEM((2, 2, 2, NZ, 16, WB // 2), bf),
             pltpu.VMEM((2, NX, 16, WA // 2), f32),
@@ -501,8 +504,8 @@
             pltpu.VMEM((2 * BLK, FFL), f32),
             pltpu.VMEM((NX * NZ, 1, 128), f32),
             pltpu.VMEM((NY * 2, 1, 128), f32),
-            pltpu.VMEM((NX, NZ, 16, WA), bf),
-            pltpu.VMEM((NX, NZ, 16, WB), bf),
+            pltpu.VMEM((NX, NZ, 16, DA), bf),
+            pltpu.VMEM((NX, NZ, 16, DB), bf),
             pltpu.VMEM((UNITS, 16, 128), bf),
             pltpu.SemaphoreType.DMA((7,)),
             pltpu.SemaphoreType.DMA((N_PHASES,)),

time: 110 us -> 104 us (0.945)
  the two profiles are of different devices: /device:TPU:16 before, /device:TPU:2 now
where the time goes in v6:
time: 104 us
  Pallas kernels  102 us (98%)
  local copies, waits for them, and re-layouts  1.82 us (2%)
    pallas_call x1, Pallas kernels, local(): pl.pallas_call(kernel, out_shape=jax.ShapeDtypeStruct((BROWS, FFL), f32),...  102 us

profile of v6, /device:TPU:2, one launch (start us, length us, event | category | flops | bytes accessed | tf_op | source)
XLA Modules:
  0.0 103.7 jit_solution(3743353299655110716)
XLA Ops:
  0.0 101.9 %galore_step.1 = f32[64,1792]{1,0:T(8,128)} custom-call(bf16[96,4096]{1,0:T(8,128)(2,1)} %tok_ref.1, bf16[768,1792]{1,0:T(8,128)(2,1)} %up_ref.1, bf16[64,512]{1,0:T(8,128)(2,1)} %basis_ref.1, f32[8,1792]{1,0:T(8,128)} %m_ref.1, f32[8,1792]{1,0:T(8,128)} %v_ref.1), custom_call_target="tpu_custom_call" | custom-call | flops 4000000000 | bytes 20000000 | tf_op jit(solution)/shard_map/galore_step/pallas_call | solution.py:476
  101.9 1.8 %copy.7 = f32[64,1792]{1,0:T(8,128)} copy(f32[64,1792]{1,0:T(8,128)} %galore_step.1) | data formatting | bytes 917504

commit v7 on v6

--- a/solution.py
+++ b/solution.py
@@ -20,7 +20,6 @@
 BROWS = 64
 X_ORDER = (0, 1, 3, 2)
 Z_ORDER = (0, 1, -1, 2, -2, 3, -3, 4)
-RZH = {1: (3, 1, 2, 0), -1: (4, -3, -1, -2)}
 SIDES = (1, -1)
 
 
@@ -196,19 +195,13 @@
             self.pass_a(j, 2, 2, (3, 4), "near")
             self.pass_a(j, -2, -2, (-3,), "near")
 
-    def step_b(self, s, prior, part):
-        comm = self.comm
-        if s and prior:
-            comm.wait(self.name_b, (0, part))
-        for n, side in enumerate(SIDES):
-            for k in RZH[side if prior else -side][2 * part:2 * part + 2]:
-                value = self.block(1, wrap(self.x + side * (2 - s), NX), self.zs(k))
-                if s and prior:
-                    value = value + self.rb[n, 0, k % NZ].astype(jnp.float32)
-                out = self.sb.at[n, s, k % NZ]
-                out[...] = value.astype(jnp.bfloat16)
-                group = (1, self.last[k]) if s else (0, part)
-                comm.send(self.name_b, group, out, self.rb.at[n, s, k % NZ], comm.dev(x=wrap(self.x + side, NX)))
+    def cross_b(self, ks):
+        for k in ks:
+            for j in (2, 1, 3):
+                xo = wrap(self.x + j, NX)
+                out = self.sb.at[j, k % NZ]
+                out[...] = self.block(1, xo, self.zs(k)).astype(jnp.bfloat16)
+                self.comm.send(self.name_b, (1, self.last[k]), out, self.rb.at[j, k % NZ], self.comm.dev(x=xo))
 
     def last_a(self):
         comm = self.comm
@@ -239,8 +232,8 @@
             comm.wait(self.name_b, ("z", ks[0]))
         for k in ks:
             value = self.block(1, self.x, self.zs(k))
-            for n in range(2):
-                value = value + self.rb[n, 1, k % NZ].astype(jnp.float32)
+            for j in (1, 2, 3):
+                value = value + self.rb[j, k % NZ].astype(jnp.float32)
             for other in plus.get(k, ()):
                 value = value + self.rbz[other % NZ].astype(jnp.float32)
             if k == 0:
@@ -252,15 +245,12 @@
             )
 
     def steps(self, begin):
-        b = self.step_b
         steps = [
-            (0.0, lambda: self.far_a(0)), (0.1, lambda: b(0, True, 0)), (0.2, lambda: self.far_a(1)),
-            (0.3, lambda: b(0, True, 1)), (0.4, lambda: self.near_a(0)), (0.5, lambda: b(1, False, 0)),
-            (0.6, lambda: self.near_a(1)), (0.7, lambda: b(1, False, 1)),
-            (3.4, lambda: self.mid_a(0)), (3.5, lambda: b(1, True, 0)),
-            (3.6, lambda: self.mid_a(1)), (3.8, lambda: b(1, True, 1)),
-            (6.9, self.last_a), (7.0, lambda: self.last_b((4, 3, -3))), (7.5, lambda: self.last_b((1, -1))),
-            (10.4, lambda: self.last_b((2, -2))),
+            (0.0, lambda: self.cross_b((4, 3, -3))), (0.1, lambda: self.far_a(0)), (0.2, lambda: self.far_a(1)),
+            (0.3, lambda: self.cross_b((1, -1))), (0.4, lambda: self.near_a(0)), (0.5, lambda: self.cross_b((2, -2))),
+            (0.6, lambda: self.near_a(1)), (0.7, lambda: self.cross_b((0,))),
+            (3.4, lambda: self.mid_a(0)), (3.6, lambda: self.mid_a(1)), (4.0, lambda: self.last_b((4, 3, -3))),
+            (5.5, lambda: self.last_b((1, -1))), (7.2, self.last_a), (7.3, lambda: self.last_b((2, -2))),
         ]
         return [(begin + t, f) for t, f in steps]
 
@@ -408,9 +398,9 @@
         ]
         tasks += scatters[q].steps(late + 24.5)
         tasks += [
-            (late + 38.0, functools.partial(finish_half, q, 1)),
+            (late + 35.6, functools.partial(finish_half, q, 1)),
             (late + 34.8, functools.partial(finish_half, q, 0)),
-            (late + 43.0, functools.partial(exchange, q)),
+            (late + 40.5, functools.partial(exchange, q)),
         ]
     run(tasks)
     g = gsum[...]
@@ -466,7 +456,7 @@
     comm.finish()
 
 
-N_PHASES, N_GROUPS = 18, 70
+N_PHASES, N_GROUPS = 18, 66
 
 
 def local(tokens, up_cotangent, basis, first_moment, second_moment):
@@ -490,8 +480,8 @@
             pltpu.VMEM((BROWS, R), bf),
             pltpu.VMEM((2, NZ, NX, 16, WA // 2), bf),
             pltpu.VMEM((2, NZ, NX, 16, WA // 2), bf),
-            pltpu.VMEM((2, 2, 2, NZ, 16, WB // 2), bf),
-            pltpu.VMEM((2, 2, 2, NZ, 16, WB // 2), bf),
+            pltpu.VMEM((2, NX, NZ, 16, WB // 2), bf),
+            pltpu.VMEM((2, NX, NZ, 16, WB // 2), bf),
             pltpu.VMEM((2, NX, 16, WA // 2), f32),
             pltpu.VMEM((2, NX, 16, WA // 2), bf),
             pltpu.VMEM((2, NX, 16, WA // 2), bf),

time: 104 us -> 104 us (level)
  no operation moved by 1% of the time
where the time goes in v7:
time: 104 us
  Pallas kernels  102 us (98%)
  local copies, waits for them, and re-layouts  1.82 us (2%)
    pallas_call x1, Pallas kernels, local(): pl.pallas_call(kernel, out_shape=jax.ShapeDtypeStruct((BROWS, FFL), f32),...  102 us

profile of v7, /device:TPU:2, one launch (start us, length us, event | category | flops | bytes accessed | tf_op | source)
XLA Modules:
  0.0 103.9 jit_solution(7764324500871787042)
XLA Ops:
  0.0 102.1 %galore_step.1 = f32[64,1792]{1,0:T(8,128)} custom-call(bf16[96,4096]{1,0:T(8,128)(2,1)} %tok_ref.1, bf16[768,1792]{1,0:T(8,128)(2,1)} %up_ref.1, bf16[64,512]{1,0:T(8,128)(2,1)} %basis_ref.1, f32[8,1792]{1,0:T(8,128)} %m_ref.1, f32[8,1792]{1,0:T(8,128)} %v_ref.1), custom_call_target="tpu_custom_call" | custom-call | flops 4000000000 | bytes 20000000 | tf_op jit(solution)/shard_map/galore_step/pallas_call | solution.py:466
  102.1 1.8 %copy.7 = f32[64,1792]{1,0:T(8,128)} copy(f32[64,1792]{1,0:T(8,128)} %galore_step.1) | data formatting | bytes 917504

commit v8 on v7

--- a/solution.py
+++ b/solution.py
@@ -12,7 +12,7 @@
 BLK = 8
 TOK = 96
 FFL = 1792
-WA, WB = 512, 1280
+WA, WB = 768, 1024
 DA, DB = 640, 1152
 R = 512
 RH = R // 2

time: 104 us -> 103 us (level)
  no operation moved by 1% of the time
where the time goes in v8:
time: 103 us
  Pallas kernels  101 us (98%)
  local copies, waits for them, and re-layouts  1.82 us (2%)
    pallas_call x1, Pallas kernels, local(): pl.pallas_call(kernel, out_shape=jax.ShapeDtypeStruct((BROWS, FFL), f32),...  101 us

profile of v8, /device:TPU:2, one launch (start us, length us, event | category | flops | bytes accessed | tf_op | source)
XLA Modules:
  0.0 103.0 jit_solution(5853909553646464001)
XLA Ops:
  0.0 101.2 %galore_step.1 = f32[64,1792]{1,0:T(8,128)} custom-call(bf16[96,4096]{1,0:T(8,128)(2,1)} %tok_ref.1, bf16[768,1792]{1,0:T(8,128)(2,1)} %up_ref.1, bf16[64,512]{1,0:T(8,128)(2,1)} %basis_ref.1, f32[8,1792]{1,0:T(8,128)} %m_ref.1, f32[8,1792]{1,0:T(8,128)} %v_ref.1), custom_call_target="tpu_custom_call" | custom-call | flops 4000000000 | bytes 20000000 | tf_op jit(solution)/shard_map/galore_step/pallas_call | solution.py:466
  101.2 1.8 %copy.7 = f32[64,1792]{1,0:T(8,128)} copy(f32[64,1792]{1,0:T(8,128)} %galore_step.1) | data formatting | bytes 917504
